TPU v7x, 512 devices: a whole 4x8x8 slice. The times are simulated.
512 devices in a mesh: dp: 64 (over z_lo, y, core), split: 8 (over x, z_hi).
Axes of the slice: x: 4, y: 8, z: 8 (z_hi: 2, z_lo: 4; z = z_hi * 4 + z_lo), core: 2. Of those that a mesh axis runs over, the one named last changes fastest.
Arguments:
- image: float32 [14336, 768], P('dp'), may hold values from -0.5 to 0.5, as said below
- text: float32 [14336, 768], P('dp'), may hold values from -0.5 to 0.5, as said below
- log_temp: float32 [1], replicated, may hold values from 1.6 to 2.4
- bias: float32 [1], replicated, may hold values from -3 to -1.5
Outputs:
- loss: float32 [], replicated
- grad_image: float32 [14336, 768], P(('dp', 'split'))
- grad_text: float32 [14336, 768], P(('dp', 'split'))
Inputs may be any that keep to these rules, and one draw needn't show every extreme that they name: Entries of the image embeddings are of order 768 ** -0.5. Entries of the text embeddings are of order 768 ** -0.5.
All inputs are finite; a program needn't handle non-finite values.
Results may differ from a plain program's by a relative error of at most 0.0003.
Values sent between devices are 32-bit elements; how exact they have to be, the bound alone decides.
A program may use at most 64 MiB of HBM per device.

v0:
```python
import jax
import jax.numpy as jnp
from jax import lax
from jax.sharding import PartitionSpec as P

EPS = 1e-06


def from_behind(block, axis, distance):
    devices = range(lax.axis_size(axis))
    route = [((i - distance) % len(devices), i) for i in devices]
    return lax.ppermute(block, axis, route)


def normalize(values):
    inverse = lax.rsqrt(jnp.sum(values * values, axis=-1, keepdims=True) + EPS)
    return (values * inverse, inverse)


def backprop_norm(grads, unit, inverse):
    return inverse * (grads - unit * jnp.sum(unit * grads, axis=-1, keepdims=True))


def local(image, text, log_temp, bias):
    groups = lax.axis_size("split")
    steps_each = lax.axis_size("dp") // groups
    member = lax.axis_index("split")
    scale = jnp.exp(log_temp[0])
    offset = bias[0]
    x_hat, inv_x = normalize(image)
    y_hat, inv_y = normalize(text)
    rows = image.shape[0]
    first_label = jnp.eye(rows, dtype=jnp.float32) * (member == 0).astype(jnp.float32)
    no_label = jnp.zeros((rows, rows), jnp.float32)
    levels = groups.bit_length() - 1
    start_block = y_hat
    for level in range(levels):
        moved = from_behind(start_block, "dp", 1 << level)
        start_block = jnp.where(member >> level & 1 == 1, moved, start_block)
    total = jnp.zeros((), jnp.float32)
    image_sum = jnp.zeros_like(x_hat)
    current = start_block
    text_sum = jnp.zeros_like(y_hat)
    for step in range(steps_each):
        label = first_label if step == 0 else no_label
        logits = scale * jnp.dot(x_hat, current.T, precision=lax.Precision.HIGHEST) + offset
        part_loss = jnp.sum(jax.nn.softplus(logits - 2.0 * label * logits))
        delta = jax.nn.sigmoid(logits) - label
        image_term = scale * jnp.dot(delta, current, precision=lax.Precision.HIGHEST)
        text_term = scale * jnp.dot(delta.T, x_hat, precision=lax.Precision.HIGHEST)
        part_loss, image_term, text_term = (part_loss, image_term, text_term)
        total = total + part_loss
        image_sum = image_sum + image_term
        text_sum = text_sum + text_term
        if step + 1 < steps_each:
            current, text_sum = from_behind((current, text_sum), "dp", groups)
        else:
            text_sum = from_behind(text_sum, "dp", groups)
    for level in range(levels):
        moved = from_behind(text_sum, "dp", -(1 << level))
        text_sum = jnp.where(member >> level & 1 == 1, moved, text_sum)
    image_share, text_share = (
        lax.psum_scatter(image_sum, "split", scatter_dimension=0, tiled=True),
        lax.psum_scatter(text_sum, "split", scatter_dimension=0, tiled=True),
    )
    share = rows // groups
    first_row = member * share
    x_rows = lax.dynamic_slice_in_dim(x_hat, first_row, share, 0)
    inv_x_rows = lax.dynamic_slice_in_dim(inv_x, first_row, share, 0)
    y_rows = lax.dynamic_slice_in_dim(y_hat, first_row, share, 0)
    inv_y_rows = lax.dynamic_slice_in_dim(inv_y, first_row, share, 0)
    grad_image = backprop_norm(image_share, x_rows, inv_x_rows)
    grad_text = backprop_norm(text_share, y_rows, inv_y_rows)
    pairs = jnp.float32(rows * lax.axis_size("dp"))
    loss = lax.psum(total, ("dp", "split")) / (pairs * pairs)
    return (loss, grad_image, grad_text)


def solution(mesh):
    in_specs = (P("dp", None), P("dp", None), P(), P())
    out_specs = (P(), P(("dp", "split"), None), P(("dp", "split"), None))
    return jax.shard_map(local, mesh=mesh, in_specs=in_specs, out_specs=out_specs, check_vma=False)
```

profile of v0, /device:TPU:2, one launch (start us, length us, event | category | flops | bytes accessed | tf_op | source)
XLA Modules:
  0.0 1201.8 jit_solution(15964877345369851828)
XLA Ops:
  2.1 1.9 collective-permute-start
  4.0 16.9 %collective-permute-done = f32[224,768]{1,0:T(8,128)S(1)} collective-permute-done((f32[224,768]{1,0:T(8,128)S(1)}, f32[224,768]{1,0:T(8,128)S(1)}, u32[]{:S(2)}, u32[]{:S(2)}) %collective-permute-start) | collective-permute-done | bytes 688160 | tf_op jit(solution)/shard_map/ppermute | solution.py:12
  21.1 1.9 collective-permute-start.1
  23.0 15.2 %collective-permute-done.1 = f32[224,768]{1,0:T(8,128)S(1)} collective-permute-done((f32[224,768]{1,0:T(8,128)S(1)}, f32[224,768]{1,0:T(8,128)S(1)}, u32[]{:S(2)}, u32[]{:S(2)}) %collective-permute-start.1) | collective-permute-done | bytes 688160 | tf_op jit(solution)/shard_map/ppermute | solution.py:12
  38.3 1.9 collective-permute-start.2
  41.9 25.4 %collective-permute-done.2 = f32[224,768]{1,0:T(8,128)S(1)} collective-permute-done((f32[224,768]{1,0:T(8,128)S(1)}, f32[224,768]{1,0:T(8,128)S(1)}, u32[]{:S(2)}, u32[]{:S(2)}) %collective-permute-start.2) | collective-permute-done | bytes 688160 | tf_op jit(solution)/shard_map/ppermute | solution.py:12
  67.3 1.9 collective-permute-start.3
  71.6 11.6 collective-permute-start.10
  83.2 42.9 %collective-permute-done.3 = f32[224,768]{1,0:T(8,128)S(1)} collective-permute-done((f32[224,768]{1,0:T(8,128)S(1)}, f32[224,768]{1,0:T(8,128)S(1)}, u32[]{:S(2)}, u32[]{:S(2)}) %collective-permute-start.3) | collective-permute-done | bytes 688160 | tf_op jit(solution)/shard_map/ppermute | solution.py:12
  126.1 1.9 collective-permute-start.4
  128.0 1.6 fusion.13
  129.5 22.8 %collective-permute-done.10 = f32[224,768]{1,0:T(8,128)S(1)} collective-permute-done((f32[224,768]{1,0:T(8,128)S(1)}, f32[224,768]{1,0:T(8,128)S(1)}, u32[]{:S(2)}, u32[]{:S(2)}) %collective-permute-start.10) | collective-permute-done | bytes 688160 | tf_op jit(solution)/shard_map/ppermute | solution.py:12
  153.1 1.9 collective-permute-start.11
  155.0 15.2 %collective-permute-done.4 = f32[224,768]{1,0:T(8,128)S(1)} collective-permute-done((f32[224,768]{1,0:T(8,128)S(1)}, f32[224,768]{1,0:T(8,128)S(1)}, u32[]{:S(2)}, u32[]{:S(2)}) %collective-permute-start.4) | collective-permute-done | bytes 688160 | tf_op jit(solution)/shard_map/ppermute | solution.py:12
  170.3 24.2 %collective-permute-start.5 = (f32[224,768]{1,0:T(8,128)S(1)}, f32[224,768]{1,0:T(8,128)S(1)}, u32[]{:S(2)}, u32[]{:S(2)}) collective-permute-start(f32[224,768]{1,0:T(8,128)S(1)} %collective-permute-done.4), channel_id=1, source_target_pairs={{448,0},{456,8},{464,16},{472,24},{480,32},{488,40},{496,48},{504,... | collective-permute-start | bytes 2064392 | tf_op jit(solution)/shard_map/ppermute | solution.py:12
  196.7 5.5 collective-permute-done.11
  202.3 8.7 collective-permute-start.12
  211.0 6.1 collective-permute-done.5
  217.0 8.7 collective-permute-start.6
  228.0 37.0 %collective-permute-done.12 = f32[224,768]{1,0:T(8,128)S(1)} collective-permute-done((f32[224,768]{1,0:T(8,128)S(1)}, f32[224,768]{1,0:T(8,128)S(1)}, u32[]{:S(2)}, u32[]{:S(2)}) %collective-permute-start.12) | collective-permute-done | bytes 688160 | tf_op jit(solution)/shard_map/ppermute | solution.py:12
  265.1 1.9 collective-permute-start.13
  267.0 24.6 %collective-permute-done.6 = f32[224,768]{1,0:T(8,128)S(1)} collective-permute-done((f32[224,768]{1,0:T(8,128)S(1)}, f32[224,768]{1,0:T(8,128)S(1)}, u32[]{:S(2)}, u32[]{:S(2)}) %collective-permute-start.6) | collective-permute-done | bytes 688160 | tf_op jit(solution)/shard_map/ppermute | solution.py:12
  291.6 15.5 %collective-permute-start.7 = (f32[224,768]{1,0:T(8,128)S(1)}, f32[224,768]{1,0:T(8,128)S(1)}, u32[]{:S(2)}, u32[]{:S(2)}) collective-permute-start(f32[224,768]{1,0:T(8,128)S(1)} %collective-permute-done.6), channel_id=1, source_target_pairs={{448,0},{456,8},{464,16},{472,24},{480,32},{488,40},{496,48},{504,... | collective-permute-start | bytes 2064392 | tf_op jit(solution)/shard_map/ppermute | solution.py:12
  307.1 1.5 fusion.16
  309.5 12.4 %collective-permute-start.14 = (f32[224,768]{1,0:T(8,128)S(1)}, f32[224,768]{1,0:T(8,128)S(1)}, u32[]{:S(2)}, u32[]{:S(2)}) collective-permute-start(f32[224,768]{1,0:T(8,128)S(1)} %add.229), channel_id=1, source_target_pairs={{448,0},{456,8},{464,16},{472,24},{480,32},{488,40},{496,48},{504,... | collective-permute-start | bytes 2064392 | tf_op jit(solution)/shard_map/ppermute | solution.py:12
  322.0 35.6 %collective-permute-done.7 = f32[224,768]{1,0:T(8,128)S(1)} collective-permute-done((f32[224,768]{1,0:T(8,128)S(1)}, f32[224,768]{1,0:T(8,128)S(1)}, u32[]{:S(2)}, u32[]{:S(2)}) %collective-permute-start.7) | collective-permute-done | bytes 688160 | tf_op jit(solution)/shard_map/ppermute | solution.py:12
  357.6 2.1 collective-permute-start.8
  359.7 1.5 fusion.17
  362.0 10.4 collective-permute-done.14
  372.5 37.0 %collective-permute-start.15 = (f32[224,768]{1,0:T(8,128)S(1)}, f32[224,768]{1,0:T(8,128)S(1)}, u32[]{:S(2)}, u32[]{:S(2)}) collective-permute-start(f32[224,768]{1,0:T(8,128)S(1)} %add.230), channel_id=1, source_target_pairs={{448,0},{456,8},{464,16},{472,24},{480,32},{488,40},{496,48},{504,... | collective-permute-start | bytes 2064392 | tf_op jit(solution)/shard_map/ppermute | solution.py:12
  409.5 4.3 collective-permute-done.8
  413.8 10.3 collective-permute-start.9
  426.4 2.2 collective-permute-done.15
  428.6 10.1 collective-permute-start.16
  438.7 39.4 %collective-permute-done.9 = f32[224,768]{1,0:T(8,128)S(1)} collective-permute-done((f32[224,768]{1,0:T(8,128)S(1)}, f32[224,768]{1,0:T(8,128)S(1)}, u32[]{:S(2)}, u32[]{:S(2)}) %collective-permute-start.9) | collective-permute-done | bytes 688160 | tf_op jit(solution)/shard_map/ppermute | solution.py:12
  480.4 12.5 %collective-permute-done.16 = f32[224,768]{1,0:T(8,128)S(1)} collective-permute-done((f32[224,768]{1,0:T(8,128)S(1)}, f32[224,768]{1,0:T(8,128)S(1)}, u32[]{:S(2)}, u32[]{:S(2)}) %collective-permute-start.16) | collective-permute-done | bytes 688160 | tf_op jit(solution)/shard_map/ppermute | solution.py:12
  492.9 3.7 collective-permute-start.17
  496.7 23.2 %collective-permute-done.17 = f32[224,768]{1,0:T(8,128)S(1)} collective-permute-done((f32[224,768]{1,0:T(8,128)S(1)}, f32[224,768]{1,0:T(8,128)S(1)}, u32[]{:S(2)}, u32[]{:S(2)}) %collective-permute-start.17) | collective-permute-done | bytes 688160 | tf_op jit(solution)/shard_map/ppermute | solution.py:12
  519.9 215.3 %collective-permute-start.18 = (f32[224,768]{1,0:T(8,128)S(1)}, f32[224,768]{1,0:T(8,128)S(1)}, u32[]{:S(2)}, u32[]{:S(2)}) collective-permute-start(f32[224,768]{1,0:T(8,128)S(1)} %collective-permute-done.17), channel_id=1, source_target_pairs={{8,0},{16,8},{24,16},{32,24},{40,32},{48,40},{56,48},{64,56},{72,6... | collective-permute-start | bytes 2064392 | tf_op jit(solution)/shard_map/ppermute | solution.py:12
  736.7 6.8 collective-permute-done.18
  743.6 18.1 %collective-permute-start.19 = (f32[224,768]{1,0:T(8,128)S(1)}, f32[224,768]{1,0:T(8,128)S(1)}, u32[]{:S(2)}, u32[]{:S(2)}) collective-permute-start(f32[224,768]{1,0:T(8,128)S(1)} %broadcast_select_fusion), channel_id=1, source_target_pairs={{16,0},{24,8},{32,16},{40,24},{48,32},{56,40},{64,48},{72,56},{80,... | collective-permute-start | bytes 2064392 | tf_op jit(solution)/shard_map/ppermute | solution.py:12
  764.1 15.3 %collective-permute-done.19 = f32[224,768]{1,0:T(8,128)S(1)} collective-permute-done((f32[224,768]{1,0:T(8,128)S(1)}, f32[224,768]{1,0:T(8,128)S(1)}, u32[]{:S(2)}, u32[]{:S(2)}) %collective-permute-start.19) | collective-permute-done | bytes 688160 | tf_op jit(solution)/shard_map/ppermute | solution.py:12
  779.5 6.5 collective-permute-start.20
  788.4 26.7 %collective-permute-done.20 = f32[224,768]{1,0:T(8,128)S(1)} collective-permute-done((f32[224,768]{1,0:T(8,128)S(1)}, f32[224,768]{1,0:T(8,128)S(1)}, u32[]{:S(2)}, u32[]{:S(2)}) %collective-permute-start.20) | collective-permute-done | bytes 688160 | tf_op jit(solution)/shard_map/ppermute | solution.py:12
  815.2 216.3 %fusion.39 = (f32[32,768]{1,0:T(8,128)S(1)}, f32[32,768]{1,0:T(8,128)S(1)}) fusion(f32[224,768]{1,0:T(8,128)S(1)} %fusion.2, f32[224,768]{1,0:T(8,128)S(1)} %broadcast_select_fusion.4), kind=kCustom, calls=%all-reduce-scatter.2 | all-reduce-scatter fusion | flops 393217 | bytes 1574912
  1031.5 4.5 collective-permute-start.22
  1036.0 6.2 collective-permute-start.21
  1049.2 148.7 %psum.7 = f32[]{:T(128)} all-reduce(f32[]{:T(128)S(6)} %add.209), channel_id=1, replica_groups=mesh['dp'=64,'split'=8] {'dp','split'}, use_global_device_ids=true, to_apply=%region_10.11 | all-reduce | flops 1 | bytes 8 | tf_op jit(solution)/shard_map/psum | solution.py:75
  (57 shorter events, 26.2 us)
Async XLA Ops:
  0.6 1.3 copy-start
  2.1 18.9 %collective-permute-start = (f32[224,768]{1,0:T(8,128)S(1)}, f32[224,768]{1,0:T(8,128)S(1)}, u32[]{:S(2)}, u32[]{:S(2)}) collective-permute-start(f32[224,768]{1,0:T(8,128)S(1)} %broadcast_multiply_fusion), channel_id=1, source_target_pairs={{504,0},{0,8},{8,16},{16,24},{24,32},{32,40},{40,48},{48,56},{56,6... | collective-permute-start | bytes 2064392 | tf_op jit(solution)/shard_map/ppermute | solution.py:12
  21.1 17.2 %collective-permute-start.1 = (f32[224,768]{1,0:T(8,128)S(1)}, f32[224,768]{1,0:T(8,128)S(1)}, u32[]{:S(2)}, u32[]{:S(2)}) collective-permute-start(f32[224,768]{1,0:T(8,128)S(1)} %broadcast_select_fusion.1), channel_id=1, source_target_pairs={{496,0},{504,8},{0,16},{8,24},{16,32},{24,40},{32,48},{40,56},{48,... | collective-permute-start | bytes 2064392 | tf_op jit(solution)/shard_map/ppermute | solution.py:12
  23.0 18.6 %copy-start.1 = (f32[224,768]{1,0:T(8,128)S(1)}, f32[224,768]{1,0:T(8,128)}, u32[]{:S(2)}) copy-start(f32[224,768]{1,0:T(8,128)} %param.4) | copy-start | bytes 2064388
  38.3 29.0 %collective-permute-start.2 = (f32[224,768]{1,0:T(8,128)S(1)}, f32[224,768]{1,0:T(8,128)S(1)}, u32[]{:S(2)}, u32[]{:S(2)}) collective-permute-start(f32[224,768]{1,0:T(8,128)S(1)} %broadcast_select_fusion.3), channel_id=1, source_target_pairs={{480,0},{488,8},{496,16},{504,24},{0,32},{8,40},{16,48},{24,56},{3... | collective-permute-start | bytes 2064392 | tf_op jit(solution)/shard_map/ppermute | solution.py:12
  67.3 58.7 %collective-permute-start.3 = (f32[224,768]{1,0:T(8,128)S(1)}, f32[224,768]{1,0:T(8,128)S(1)}, u32[]{:S(2)}, u32[]{:S(2)}) collective-permute-start(f32[224,768]{1,0:T(8,128)S(1)} %broadcast_select_fusion.5), channel_id=1, source_target_pairs={{448,0},{456,8},{464,16},{472,24},{480,32},{488,40},{496,48},{504,... | collective-permute-start | bytes 2064392 | tf_op jit(solution)/shard_map/ppermute | solution.py:12
  71.6 80.8 %collective-permute-start.10 = (f32[224,768]{1,0:T(8,128)S(1)}, f32[224,768]{1,0:T(8,128)S(1)}, u32[]{:S(2)}, u32[]{:S(2)}) collective-permute-start(f32[224,768]{1,0:T(8,128)S(1)} %convolution_multiply_fusion.7), channel_id=1, source_target_pairs={{448,0},{456,8},{464,16},{472,24},{480,32},{488,40},{496,48},{504,... | collective-permute-start | bytes 2064392 | tf_op jit(solution)/shard_map/ppermute | solution.py:12
  126.1 44.2 %collective-permute-start.4 = (f32[224,768]{1,0:T(8,128)S(1)}, f32[224,768]{1,0:T(8,128)S(1)}, u32[]{:S(2)}, u32[]{:S(2)}) collective-permute-start(f32[224,768]{1,0:T(8,128)S(1)} %collective-permute-done.3), channel_id=1, source_target_pairs={{448,0},{456,8},{464,16},{472,24},{480,32},{488,40},{496,48},{504,... | collective-permute-start | bytes 2064392 | tf_op jit(solution)/shard_map/ppermute | solution.py:12
  153.1 49.1 %collective-permute-start.11 = (f32[224,768]{1,0:T(8,128)S(1)}, f32[224,768]{1,0:T(8,128)S(1)}, u32[]{:S(2)}, u32[]{:S(2)}) collective-permute-start(f32[224,768]{1,0:T(8,128)S(1)} %fusion.3), channel_id=1, source_target_pairs={{448,0},{456,8},{464,16},{472,24},{480,32},{488,40},{496,48},{504,... | collective-permute-start | bytes 2064392 | tf_op jit(solution)/shard_map/ppermute | solution.py:12
  170.3 46.8 %collective-permute-start.5 = (f32[224,768]{1,0:T(8,128)S(1)}, f32[224,768]{1,0:T(8,128)S(1)}, u32[]{:S(2)}, u32[]{:S(2)}) collective-permute-start(f32[224,768]{1,0:T(8,128)S(1)} %collective-permute-done.4), channel_id=1, source_target_pairs={{448,0},{456,8},{464,16},{472,24},{480,32},{488,40},{496,48},{504,... | collective-permute-start | bytes 2064392 | tf_op jit(solution)/shard_map/ppermute | solution.py:12
  202.3 62.7 %collective-permute-start.12 = (f32[224,768]{1,0:T(8,128)S(1)}, f32[224,768]{1,0:T(8,128)S(1)}, u32[]{:S(2)}, u32[]{:S(2)}) collective-permute-start(f32[224,768]{1,0:T(8,128)S(1)} %add.227), channel_id=1, source_target_pairs={{448,0},{456,8},{464,16},{472,24},{480,32},{488,40},{496,48},{504,... | collective-permute-start | bytes 2064392 | tf_op jit(solution)/shard_map/ppermute | solution.py:12
  217.0 74.6 %collective-permute-start.6 = (f32[224,768]{1,0:T(8,128)S(1)}, f32[224,768]{1,0:T(8,128)S(1)}, u32[]{:S(2)}, u32[]{:S(2)}) collective-permute-start(f32[224,768]{1,0:T(8,128)S(1)} %collective-permute-done.5), channel_id=1, source_target_pairs={{448,0},{456,8},{464,16},{472,24},{480,32},{488,40},{496,48},{504,... | collective-permute-start | bytes 2064392 | tf_op jit(solution)/shard_map/ppermute | solution.py:12
  265.1 44.4 %collective-permute-start.13 = (f32[224,768]{1,0:T(8,128)S(1)}, f32[224,768]{1,0:T(8,128)S(1)}, u32[]{:S(2)}, u32[]{:S(2)}) collective-permute-start(f32[224,768]{1,0:T(8,128)S(1)} %add.228), channel_id=1, source_target_pairs={{448,0},{456,8},{464,16},{472,24},{480,32},{488,40},{496,48},{504,... | collective-permute-start | bytes 2064392 | tf_op jit(solution)/shard_map/ppermute | solution.py:12
  291.6 66.0 %collective-permute-start.7 = (f32[224,768]{1,0:T(8,128)S(1)}, f32[224,768]{1,0:T(8,128)S(1)}, u32[]{:S(2)}, u32[]{:S(2)}) collective-permute-start(f32[224,768]{1,0:T(8,128)S(1)} %collective-permute-done.6), channel_id=1, source_target_pairs={{448,0},{456,8},{464,16},{472,24},{480,32},{488,40},{496,48},{504,... | collective-permute-start | bytes 2064392 | tf_op jit(solution)/shard_map/ppermute | solution.py:12
  309.5 62.9 %collective-permute-start.14 = (f32[224,768]{1,0:T(8,128)S(1)}, f32[224,768]{1,0:T(8,128)S(1)}, u32[]{:S(2)}, u32[]{:S(2)}) collective-permute-start(f32[224,768]{1,0:T(8,128)S(1)} %add.229), channel_id=1, source_target_pairs={{448,0},{456,8},{464,16},{472,24},{480,32},{488,40},{496,48},{504,... | collective-permute-start | bytes 2064392 | tf_op jit(solution)/shard_map/ppermute | solution.py:12
  357.6 56.2 %collective-permute-start.8 = (f32[224,768]{1,0:T(8,128)S(1)}, f32[224,768]{1,0:T(8,128)S(1)}, u32[]{:S(2)}, u32[]{:S(2)}) collective-permute-start(f32[224,768]{1,0:T(8,128)S(1)} %collective-permute-done.7), channel_id=1, source_target_pairs={{448,0},{456,8},{464,16},{472,24},{480,32},{488,40},{496,48},{504,... | collective-permute-start | bytes 2064392 | tf_op jit(solution)/shard_map/ppermute | solution.py:12
  372.5 56.0 %collective-permute-start.15 = (f32[224,768]{1,0:T(8,128)S(1)}, f32[224,768]{1,0:T(8,128)S(1)}, u32[]{:S(2)}, u32[]{:S(2)}) collective-permute-start(f32[224,768]{1,0:T(8,128)S(1)} %add.230), channel_id=1, source_target_pairs={{448,0},{456,8},{464,16},{472,24},{480,32},{488,40},{496,48},{504,... | collective-permute-start | bytes 2064392 | tf_op jit(solution)/shard_map/ppermute | solution.py:12
  413.8 64.4 %collective-permute-start.9 = (f32[224,768]{1,0:T(8,128)S(1)}, f32[224,768]{1,0:T(8,128)S(1)}, u32[]{:S(2)}, u32[]{:S(2)}) collective-permute-start(f32[224,768]{1,0:T(8,128)S(1)} %collective-permute-done.8), channel_id=1, source_target_pairs={{448,0},{456,8},{464,16},{472,24},{480,32},{488,40},{496,48},{504,... | collective-permute-start | bytes 2064392 | tf_op jit(solution)/shard_map/ppermute | solution.py:12
  428.6 64.2 %collective-permute-start.16 = (f32[224,768]{1,0:T(8,128)S(1)}, f32[224,768]{1,0:T(8,128)S(1)}, u32[]{:S(2)}, u32[]{:S(2)}) collective-permute-start(f32[224,768]{1,0:T(8,128)S(1)} %add.231), channel_id=1, source_target_pairs={{448,0},{456,8},{464,16},{472,24},{480,32},{488,40},{496,48},{504,... | collective-permute-start | bytes 2064392 | tf_op jit(solution)/shard_map/ppermute | solution.py:12
  492.9 26.9 %collective-permute-start.17 = (f32[224,768]{1,0:T(8,128)S(1)}, f32[224,768]{1,0:T(8,128)S(1)}, u32[]{:S(2)}, u32[]{:S(2)}) collective-permute-start(f32[224,768]{1,0:T(8,128)S(1)} %add.232), channel_id=1, source_target_pairs={{448,0},{456,8},{464,16},{472,24},{480,32},{488,40},{496,48},{504,... | collective-permute-start | bytes 2064392 | tf_op jit(solution)/shard_map/ppermute | solution.py:12
  519.9 223.7 %collective-permute-start.18 = (f32[224,768]{1,0:T(8,128)S(1)}, f32[224,768]{1,0:T(8,128)S(1)}, u32[]{:S(2)}, u32[]{:S(2)}) collective-permute-start(f32[224,768]{1,0:T(8,128)S(1)} %collective-permute-done.17), channel_id=1, source_target_pairs={{8,0},{16,8},{24,16},{32,24},{40,32},{48,40},{56,48},{64,56},{72,6... | collective-permute-start | bytes 2064392 | tf_op jit(solution)/shard_map/ppermute | solution.py:12
  743.6 35.8 %collective-permute-start.19 = (f32[224,768]{1,0:T(8,128)S(1)}, f32[224,768]{1,0:T(8,128)S(1)}, u32[]{:S(2)}, u32[]{:S(2)}) collective-permute-start(f32[224,768]{1,0:T(8,128)S(1)} %broadcast_select_fusion), channel_id=1, source_target_pairs={{16,0},{24,8},{32,16},{40,24},{48,32},{56,40},{64,48},{72,56},{80,... | collective-permute-start | bytes 2064392 | tf_op jit(solution)/shard_map/ppermute | solution.py:12
  779.5 35.6 %collective-permute-start.20 = (f32[224,768]{1,0:T(8,128)S(1)}, f32[224,768]{1,0:T(8,128)S(1)}, u32[]{:S(2)}, u32[]{:S(2)}) collective-permute-start(f32[224,768]{1,0:T(8,128)S(1)} %broadcast_select_fusion.2), channel_id=1, source_target_pairs={{32,0},{40,8},{48,16},{56,24},{64,32},{72,40},{80,48},{88,56},{96,... | collective-permute-start | bytes 2064392 | tf_op jit(solution)/shard_map/ppermute | solution.py:12
  1031.5 167.0 %collective-permute-start.22 = (f32[28,768]{1,0:T(8,128)S(1)}, f32[28,768]{1,0:T(8,128)S(1)}, u32[]{:S(2)}, u32[]{:S(2)}) collective-permute-start(f32[28,768]{1,0:T(8,128)S(1)} %slice.1), channel_id=1, source_target_pairs={{0,1},{1,2},{2,3},{3,4},{4,5},{5,6},{6,7},{8,9},{9,10},{10,11},{11... | collective-permute-start | bytes 258056
  1036.0 162.9 %collective-permute-start.21 = (f32[28,768]{1,0:T(8,128)S(1)}, f32[28,768]{1,0:T(8,128)S(1)}, u32[]{:S(2)}, u32[]{:S(2)}) collective-permute-start(f32[28,768]{1,0:T(8,128)S(1)} %slice), channel_id=1, source_target_pairs={{0,1},{1,2},{2,3},{3,4},{4,5},{5,6},{6,7},{8,9},{9,10},{10,11},{11... | collective-permute-start | bytes 258056
where the time goes:
time: 1200 us
  starting transfers between devices  408 us (34%)
  waiting for transfers between devices  388 us (32%)
  blocking collectives  365 us (30%)
  matrix products  24.6 us (2%)
    ppermute x21, starting transfers between devices, from_behind(): return lax.ppermute(block, axis, route)  398 us
    ppermute x21, waiting for transfers between devices, from_behind(): return lax.ppermute(block, axis, route)  388 us
    unnamed x1, blocking collectives  216 us
    psum x1, blocking collectives, local(): loss = lax.psum(total, ('dp', 'split')) / (pairs * pairs)  149 us
  transfers between devices with their start and end apart: 23, of which 20 were waited for; matrix products, arithmetic and copies ran while one was open for 2% of the time, Pallas kernels for 0%

commit v1 on v0

v1 whole, which is shorter than its diff:
```python
import functools

import jax
import jax.numpy as jnp
from jax import lax
from jax.experimental import pallas as pl
from jax.experimental.pallas import tpu as pltpu
from jax.sharding import PartitionSpec as P

EPS = 1e-06
MESH = pl.DeviceIdType.MESH
D = 768
NX, NY, NZ, NL = 4, 8, 8, 4
SHARE = 28
PAD = 32
BLOCK = 224
TEXT = 56
S = NX * NL * PAD
T = 2 * NY * TEXT
HALF = D // 2
NC = 3
CC = D // NC
TILE = 128
F32 = jnp.float32
BF16 = jnp.bfloat16


def split_bf16(v):
    hi = v.astype(BF16)
    return hi, (v - hi.astype(F32)).astype(BF16)


def dot(a, b, ca, cb):
    return lax.dot_general(a, b, (((ca,), (cb,)), ((), ())), preferred_element_type=F32)


def kernel(
    img, txt, lt_ref, bias_ref,
    loss_o, gi_o, gt_o,
    xh, invx, xs, ys, xb_hi, xb_lo, yb_hi, yb_lo, d_hi, d_lo,
    gy, gy_in, rs_in, gz, gz_in, gxs, xr, zs, zr, lacc, lc, lx, ly, lz, lm,
    z_ss, z_rs, ag_ss, ag_rs, co_ss, co_rs, gc_ss, gc_rs, rs_ss, rs_rs,
    h_ss, h_rs, x_ss, x_rs, q_ss, q_rs, lc_ss, lc_rs, lx_ss, lx_rs, ly_ss, ly_rs, lz_ss, lz_rs,
):
    dp = lax.axis_index("dp")
    split = lax.axis_index("split")
    k = lax.rem(dp, 2)
    y = lax.rem(lax.div(dp, 2), NY)
    zl = lax.div(dp, 2 * NY)
    x = lax.div(split, 2)
    zh = lax.rem(split, 2)
    z = zh * NL + zl

    def dev(x_, y_, z_, k_):
        return (lax.rem(z_, NL) * (2 * NY) + y_ * 2 + k_, x_ * 2 + lax.div(z_, NL))

    def at_x(d):
        return dev(lax.rem(x + d, NX), y, z, k)

    def at_y(d):
        return dev(x, lax.rem(y + d, NY), z, k)

    def at_z(d):
        return dev(x, y, lax.rem(z + d, NZ), k)

    other = dev(x, y, z, 1 - k)

    def at_line(r):
        return dev(x, y, zh * NL + lax.rem(zl + r, NL), k)

    def rcopy(src, dst, ss, rs, to):
        return pltpu.make_async_remote_copy(src, dst, ss, rs, device_id=to, device_id_type=MESH)

    barrier = pltpu.get_barrier_semaphore()
    partners = [at_x(d) for d in range(1, NX)] + [at_y(d) for d in range(1, NY)]
    partners += [at_z(d) for d in range(1, NZ)] + [other]
    for to in partners:
        pl.semaphore_signal(barrier, inc=1, device_id=to, device_id_type=MESH)

    for s in range(2 * NX):
        v = img[SHARE * s : SHARE * (s + 1), :]
        inv = lax.rsqrt(jnp.sum(v * v, axis=-1, keepdims=True) + EPS)
        xh[s % 2, s // 2] = v * inv
        invx[s % 2, s // 2] = jnp.broadcast_to(inv, (SHARE, 128))
    v = txt[pl.ds(pl.multiple_of(x * TEXT, 8), TEXT), :]
    inv_y = lax.rsqrt(jnp.sum(v * v, axis=-1, keepdims=True) + EPS)
    ys[0:TEXT, :] = v * inv_y

    pl.semaphore_wait(barrier, len(partners))

    def trow(kk, dy):
        return pl.ds(kk * NY * TEXT + dy * TEXT, TEXT)

    def cols(h):
        return pl.ds(h * HALF, HALF)

    def ag(h, right, s):
        if right:
            src, dst, to = (NY - (s - 1)) % NY, NY - s, at_y(1)
        else:
            src, dst, to = s - 1, s, at_y(NY - 1)
        i = h * 8 + (0 if right else 4) + s - 1
        return rcopy(ys.at[trow(0, src), cols(h)], ys.at[trow(0, dst), cols(h)], ag_ss.at[i], ag_rs.at[i], to)

    def core_copy(dy, h):
        i = dy * 2 + h
        return rcopy(ys.at[trow(0, dy), cols(h)], ys.at[trow(1, dy), cols(h)], co_ss.at[i], co_rs.at[i], other)

    def steps(h, right):
        return NY // 2 if right == (h == 0) else NY // 2 - 1

    order = [(h, right) for h in range(2) for right in (True, False)]
    for h, right in order:
        ag(h, right, 1).start()

    def zcopy(d):
        there = lax.div(lax.rem(z + d, NZ), NL)
        if d == 1:
            return rcopy(xh.at[there], xs.at[2], z_ss.at[0], z_rs.at[0], at_z(1))
        if d == NZ - 1:
            return rcopy(xh.at[there], xs.at[0], z_ss.at[1], z_rs.at[1], at_z(NZ - 1))
        half = 0 if d == 2 else 1
        part = pl.ds(half * 2, 2)
        return rcopy(xh.at[there, part], xs.at[1, part], z_ss.at[2 + half], z_rs.at[2 + half], at_z(d))

    zcopies = [zcopy(d) for d in (1, NZ - 1, 2, NZ - 2)]
    for c in zcopies:
        c.start()
    core_copies = []
    for h in range(2):
        c = core_copy(0, h)
        c.start()
        core_copies.append(c)

    xb_hi[...] = jnp.zeros_like(xb_hi)
    xb_lo[...] = jnp.zeros_like(xb_lo)

    def put(r, block):
        for j in range(NX):
            hi, lo = split_bf16(block(j))
            row = (j * NL + r) * PAD
            xb_hi[row : row + SHARE, :] = hi
            xb_lo[row : row + SHARE, :] = lo

    put(0, lambda j: xh[zh, j])

    for s in range(1, NY // 2 + 1):
        for h, right in order:
            if s <= steps(h, right):
                ag(h, right, s).wait_recv()
                if s < steps(h, right):
                    ag(h, right, s + 1).start()
                c = core_copy(NY - s if right else s, h)
                c.start()
                core_copies.append(c)
    for c in zcopies:
        c.wait()
    for r in range(1, NL):
        put(r, lambda j: xs[r - 1, j])
    for c in core_copies:
        c.wait()
    for h, right in order:
        for s in range(1, steps(h, right) + 1):
            ag(h, right, s).wait_send()

    scale = jnp.exp(jnp.full((1, S), lt_ref[0], F32))
    offset = bias_ref[0]
    lacc[...] = jnp.zeros_like(lacc)

    def cast_tile(i, carry):
        rows = pl.ds(pl.multiple_of(i * TILE, TILE), TILE)
        hi, lo = split_bf16(ys[rows, :])
        yb_hi[rows, :] = hi
        yb_lo[rows, :] = lo
        return carry

    lax.fori_loop(0, T // TILE, cast_tile, 0)

    def pair_tile(i, carry):
        rows = pl.ds(pl.multiple_of(i * TILE, TILE), TILE)
        yh, yl = yb_hi[rows, :], yb_lo[rows, :]
        prod = dot(yh, xb_hi[...], 1, 1) + (dot(yl, xb_hi[...], 1, 1) + dot(yh, xb_lo[...], 1, 1))
        logits = scale * prod + offset
        u = jnp.exp(-jnp.abs(logits))
        w = 1.0 + u
        r = 1.0 / w
        sp = jnp.maximum(logits, 0.0) + (jnp.log(w) + (u - (w - 1.0)) * r)
        sig = jnp.where(logits >= 0.0, r, u * r)
        lacc[...] += jnp.sum(sp.reshape(TILE // 8, 8, S), axis=0)
        hi, lo = split_bf16(sig)
        gy[rows, :] = dot(hi, xb_hi[...], 1, 0) + (dot(lo, xb_hi[...], 1, 0) + dot(hi, xb_lo[...], 1, 0))
        hi, lo = split_bf16(sig.T)
        d_hi[:, rows] = hi
        d_lo[:, rows] = lo
        return carry

    lax.fori_loop(0, T // TILE, pair_tile, 0)

    def gcopy(dy):
        return rcopy(gy.at[trow(1, dy), :], gy_in.at[pl.ds(dy * TEXT, TEXT), :], gc_ss.at[dy], gc_rs.at[dy], other)

    far_first = (4, 3, 5, 2, 6, 1, 7, 0)
    for dy in far_first:
        gcopy(dy).start()

    x_own = xh[zh, x]
    y_all = ys[0:TEXT, :]
    y_own = jnp.where(zh == 0, y_all[0:SHARE, :], y_all[SHARE:TEXT, :])
    iy_own = jnp.where(zh == 0, inv_y[0:SHARE, :], inv_y[SHARE:TEXT, :])
    scale1 = scale[:, 0:1]
    lane = lax.broadcasted_iota(jnp.int32, (8, S), 1)
    pairs = jnp.sum(jnp.where(lax.rem(lane, PAD) < SHARE, lacc[...], 0.0))
    same = jnp.sum(jnp.sum(x_own * y_own, axis=-1, keepdims=True) * scale1 + offset)
    lc[k] = jnp.full((8, 128), pairs - same, F32)

    def lsend(buf, me, ss, rs, to, n):
        copies = [rcopy(buf.at[me], buf.at[me], ss.at[d - 1], rs.at[d - 1], to(d)) for d in range(1, n)]
        for c in copies:
            c.start()
        return copies

    def lsum(buf, copies, n):
        for c in copies:
            c.wait()
        out = buf[0]
        for i in range(1, n):
            out = out + buf[i]
        return out

    lcopies = lsend(lc, k, lc_ss, lc_rs, lambda d: other, 2)

    def xcopy(c, d):
        i = c * 3 + d - 1
        return rcopy(gxs.at[c, lax.rem(x + d, NX)], xr.at[c, d - 1], x_ss.at[i], x_rs.at[i], at_x(d))

    def image_sums(c):
        yh, yl = yb_hi[:, c * CC : (c + 1) * CC], yb_lo[:, c * CC : (c + 1) * CC]

        def one(j, carry):
            rows = pl.ds(pl.multiple_of(j * TILE, TILE), TILE)
            dh, dl = d_hi[rows, :], d_lo[rows, :]
            g = dot(dh, yh, 1, 0) + (dot(dl, yh, 1, 0) + dot(dh, yl, 1, 0))
            for r in range(NL):
                gxs[c, j, r] = g[r * PAD : r * PAD + SHARE, :]
            return carry

        lax.fori_loop(0, NX, one, 0)
        for d in range(1, NX):
            xcopy(c, d).start()

    def rs(h, right, s):
        n = steps(h, right)
        dist = n - s + 1
        dy = dist if right else NY - dist
        i = h * 8 + (0 if right else 4) + s - 1
        return rcopy(
            gy.at[trow(0, dy), cols(h)], rs_in.at[i], rs_ss.at[i], rs_rs.at[i], at_y(1 if right else NY - 1)
        )

    image_sums(0)
    for dy in far_first:
        gcopy(dy).wait()
        rows = pl.ds(dy * TEXT, TEXT)
        gy[rows, :] = gy[rows, :] + gy_in[rows, :]
        for h, right in order:
            n = steps(h, right)
            if dy == (n if right else NY - n):
                rs(h, right, 1).start()
    image_sums(1)
    image_sums(2)
    lx[x] = lsum(lc, lcopies, 2)
    lcopies = lsend(lx, x, lx_ss, lx_rs, at_x, NX)

    def qcopy(c, r):
        i = c * 3 + r - 1
        return rcopy(zs.at[c, r], zr.at[c, r - 1], q_ss.at[i], q_rs.at[i], at_line(r))

    def x_done(c):
        for d in range(1, NX):
            xcopy(c, d).wait()
        zs[c] = gxs[c, x] + xr[c, 0] + xr[c, 1] + xr[c, 2]
        for r in range(1, NL):
            qcopy(c, r).start()

    def rs_step(s):
        for h, right in order:
            n = steps(h, right)
            if s <= n:
                rs(h, right, s).wait_recv()
                dist = n - s
                dy = 0 if dist == 0 else (dist if right else NY - dist)
                i = h * 8 + (0 if right else 4) + s - 1
                gy[dy * TEXT : (dy + 1) * TEXT, h * HALF : (h + 1) * HALF] += rs_in[i]
                if s < n:
                    rs(h, right, s + 1).start()

    rs_step(1)
    ly[y] = lsum(lx, lcopies, NX)
    lcopies = lsend(ly, y, ly_ss, ly_rs, at_y, NY)
    x_done(0)
    rs_step(2)
    lz[z] = lsum(ly, lcopies, NY)
    lcopies = lsend(lz, z, lz_ss, lz_rs, at_z, NZ)
    x_done(1)
    rs_step(3)
    x_done(2)
    rs_step(4)
    gz[0] = gy[0:SHARE, :]
    gz[1] = gy[SHARE:TEXT, :]
    hcopy = rcopy(gz.at[1 - zh], gz_in, h_ss, h_rs, at_z(NL))
    hcopy.start()
    loss_o[...] = lsum(lz, lcopies, NZ) * (1.0 / float(BLOCK * 2 * NY * NL) ** 2)

    for c in range(NC):
        for r in range(1, NL):
            qcopy(c, r).wait()
        lm[:, c * CC : (c + 1) * CC] = zs[c, 0] + zr[c, 0] + zr[c, 1] + zr[c, 2]
    g = scale1 * (lm[...] - y_own)
    gi_o[...] = invx[zh, x][:, 0:1] * (g - x_own * jnp.sum(x_own * g, axis=-1, keepdims=True))

    hcopy.wait()
    g = scale1 * (gz[zh] + gz_in[...] - x_own)
    gt_o[...] = iy_own * (g - y_own * jnp.sum(y_own * g, axis=-1, keepdims=True))

    for h, right in order:
        for s in range(1, steps(h, right) + 1):
            rs(h, right, s).wait_send()


def local(image, text, log_temp, bias):
    vmem = pl.BlockSpec(memory_space=pltpu.VMEM)
    smem = pl.BlockSpec(memory_space=pltpu.SMEM)
    dma = pltpu.SemaphoreType.DMA
    scratch = [
        pltpu.VMEM((2, NX, SHARE, D), F32),
        pltpu.VMEM((2, NX, SHARE, 128), F32),
        pltpu.VMEM((NL - 1, NX, SHARE, D), F32),
        pltpu.VMEM((T, D), F32),
        pltpu.VMEM((S, D), BF16),
        pltpu.VMEM((S, D), BF16),
        pltpu.VMEM((T, D), BF16),
        pltpu.VMEM((T, D), BF16),
        pltpu.VMEM((S, T), BF16),
        pltpu.VMEM((S, T), BF16),
        pltpu.VMEM((T, D), F32),
        pltpu.VMEM((T // 2, D), F32),
        pltpu.VMEM((16, TEXT, HALF), F32),
        pltpu.VMEM((2, SHARE, D), F32),
        pltpu.VMEM((SHARE, D), F32),
        pltpu.VMEM((NC, NX, NL, SHARE, CC), F32),
        pltpu.VMEM((NC, NX - 1, NL, SHARE, CC), F32),
        pltpu.VMEM((NC, NL, SHARE, CC), F32),
        pltpu.VMEM((NC, NL - 1, SHARE, CC), F32),
        pltpu.VMEM((8, S), F32),
        pltpu.VMEM((2, 8, 128), F32),
        pltpu.VMEM((NX, 8, 128), F32),
        pltpu.VMEM((NY, 8, 128), F32),
        pltpu.VMEM((NZ, 8, 128), F32),
        pltpu.VMEM((SHARE, D), F32),
    ]
    for n in (4, 16, 16, 8, 16):
        scratch += [dma((n,)), dma((n,))]
    scratch += [dma, dma]
    for n in (3 * NC, 3 * NC, 1, NX - 1, NY - 1, NZ - 1):
        scratch += [dma((n,)), dma((n,))]
    loss, gi, gt = pl.pallas_call(
        kernel,
        out_shape=(
            jax.ShapeDtypeStruct((8, 128), F32),
            jax.ShapeDtypeStruct((SHARE, D), F32),
            jax.ShapeDtypeStruct((SHARE, D), F32),
        ),
        in_specs=[vmem, vmem, smem, smem],
        out_specs=(vmem, vmem, vmem),
        scratch_shapes=scratch,
        compiler_params=pltpu.CompilerParams(
            collective_id=0, has_side_effects=True, vmem_limit_bytes=48 << 20
        ),
    )(image, text, log_temp, bias)
    return loss[0, 0], gi, gt


def solution(mesh):
    in_specs = (P("dp", None), P("dp", None), P(), P())
    out_specs = (P(), P(("dp", "split"), None), P(("dp", "split"), None))
    return jax.shard_map(local, mesh=mesh, in_specs=in_specs, out_specs=out_specs, check_vma=False)
```

time: 1200 us -> 90.2 us (0.08)
  the two profiles are of different devices: /device:TPU:2 before, /device:TPU:128 now
where the time goes in v1:
time: 90.2 us; the launch traced here: 89.9 us
  Pallas kernels  84 us (93%)
  local copies, waits for them, and re-layouts  3.98 us (4%)
  between operations  1.94 us (2%)
    pallas_call x1, Pallas kernels, local(): pl.pallas_call(kernel, out_shape=(jax.ShapeDtypeStruct((8, 128), F32), ja...  84 us
    unnamed x6, local copies, waits for them, and re-layouts  3.47 us

profile of v1, /device:TPU:128, one launch (start us, length us, event | category | flops | bytes accessed | tf_op | source)
XLA Modules:
  0.0 89.9 jit_solution(14266112973744923981)
XLA Ops:
  1.9 0.0 copy-start
  1.9 1.1 %copy-done = f32[224,768]{1,0:T(8,128)S(1)} copy-done((f32[224,768]{1,0:T(8,128)S(1)}, f32[224,768]{1,0:T(8,128)}, u32[]{:S(2)}) %copy-start) | copy-done | bytes 688152
  3.0 0.0 copy-start.1
  3.0 1.1 %copy-done.1 = f32[224,768]{1,0:T(8,128)S(1)} copy-done((f32[224,768]{1,0:T(8,128)S(1)}, f32[224,768]{1,0:T(8,128)}, u32[]{:S(2)}) %copy-start.1) | copy-done | bytes 688152
  4.1 84.0 %shard_map.67 = (f32[8,128]{1,0:T(8,128)S(1)}, f32[28,768]{1,0:T(8,128)S(1)}, f32[28,768]{1,0:T(8,128)S(1)}) custom-call(f32[224,768]{1,0:T(8,128)S(1)} %copy-done, f32[224,768]{1,0:T(8,128)S(1)} %copy-done.1, f32[1]{0:T(128)S(6)} %copy.9.lt_ref, f32[1]{0:T(128)S(6)} %copy.10.bias_ref), custom_call_target="tpu_custom_call" | custom-call | tf_op jit(solution)/shard_map/pallas_call | solution.py:366
  88.1 0.5 slice.3
  88.7 0.6 copy.11
  89.3 0.6 copy.12
Async XLA Ops:
  1.9 1.1 %copy-start = (f32[224,768]{1,0:T(8,128)S(1)}, f32[224,768]{1,0:T(8,128)}, u32[]{:S(2)}) copy-start(f32[224,768]{1,0:T(8,128)} %img.1) | copy-start | bytes 2064388
  3.0 1.1 %copy-start.1 = (f32[224,768]{1,0:T(8,128)S(1)}, f32[224,768]{1,0:T(8,128)}, u32[]{:S(2)}) copy-start(f32[224,768]{1,0:T(8,128)} %txt.1) | copy-start | bytes 2064388

commit v2 on v0

v2 whole, which is shorter than its diff:
```python
import jax
import jax.numpy as jnp
from jax import lax
from jax.experimental import pallas as pl
from jax.experimental.pallas import tpu as pltpu
from jax.sharding import PartitionSpec as P

EPS = 1e-06
MESH = pl.DeviceIdType.MESH
D = 768
NX, NY, NZ, NL = 4, 8, 8, 4
N = 14336
SHARE = 28
BLOCK = 224
TEXT = 56
S = 4 * BLOCK
T = NY * TEXT
HALF = D // 2
NC = 3
CC = D // NC
TT = T // 2
F32 = jnp.float32
BF16 = jnp.bfloat16
SLOT = {1: 0, 7: 1, 2: 2, 6: 3, 3: 4, 5: 5, 0: 6, 4: 7}


def split_bf16(v):
    hi = v.astype(BF16)
    return hi, (v - hi.astype(F32)).astype(BF16)


def dot3(ah, al, bh, bl, ca, cb):
    def one(a, b):
        return lax.dot_general(a, b, (((ca,), (cb,)), ((), ())), preferred_element_type=F32)

    return one(ah, bh) + one(al, bh) + one(ah, bl)


def unit_rows(v):
    inv = lax.rsqrt(jnp.sum(v * v, axis=-1, keepdims=True) + EPS)
    return v * inv, inv


def kernel(
    img_hbm, txt_hbm, lt_ref, bias_ref,
    loss_o, gi_o, gt_o,
    img, txt, xo, yo, xs, ys, xb_hi, xb_lo, yb_hi, yb_lo, d_hi, d_lo,
    gy, ge_in, gf_in, rs_in, gz, gz_in, gt, gxs, gc_in, xa_in, xf_in, zs, zr, gx, lacc, lc, lx, ly, lz,
    in_s, e_ss, e_rs, ag_ss, ag_rs, ic_ss, ic_rs, iz_ss, iz_rs, ix_ss, ix_rs,
    ge_ss, ge_rs, rs_ss, rs_rs, gc_ss, gc_rs, xa_ss, xa_rs, xf_ss, xf_rs, q_ss, q_rs, h_ss, h_rs,
    lc_ss, lc_rs, lx_ss, lx_rs, ly_ss, ly_rs, lz_ss, lz_rs,
):
    dp = lax.axis_index("dp")
    split = lax.axis_index("split")
    k = lax.rem(dp, 2)
    y = lax.rem(lax.div(dp, 2), NY)
    zl = lax.div(dp, 2 * NY)
    x = lax.div(split, 2)
    zh = lax.rem(split, 2)
    z = zh * NL + zl
    odd = lax.rem(z, 2)
    zp = z + 1 - 2 * odd
    zq = lax.rem(z + 7 - 6 * odd, NZ)
    inner = jnp.where(jnp.logical_and(z >= 3, z <= 6), 1, 0)
    own = k == lax.rem(odd + inner, 2)
    guest = jnp.logical_not(own)

    def dev(x_, y_, z_, k_):
        return (lax.rem(z_, NL) * (2 * NY) + y_ * 2 + k_, x_ * 2 + lax.div(z_, NL))

    def at_x(d):
        return dev(lax.rem(x + d, NX), y, z, k)

    def at_y(d):
        return dev(x, lax.rem(y + d, NY), z, k)

    def at_z(z_):
        return dev(x, y, lax.rem(z_, NZ), k)

    other = dev(x, y, z, 1 - k)

    def rcopy(src, dst, ss, rs, to):
        return pltpu.make_async_remote_copy(src, dst, ss, rs, device_id=to, device_id_type=MESH)

    own_rows = pl.ds(pl.multiple_of(x * TEXT, 8), TEXT)
    in_img = pltpu.make_async_copy(img_hbm, img, in_s.at[0])
    in_txt = pltpu.make_async_copy(txt_hbm.at[own_rows, :], txt, in_s.at[1])
    in_txt.start()
    in_img.start()
    barrier = pltpu.get_barrier_semaphore()
    partners = [at_x(d) for d in range(1, NX)] + [at_y(d) for d in range(1, NY)]
    partners += [at_z(z + d) for d in range(1, NZ)] + [other]
    for to in partners:
        pl.semaphore_signal(barrier, inc=1, device_id=to, device_id_type=MESH)

    def trow(dy):
        return pl.ds(SLOT[dy] * TEXT, TEXT)

    def cols(h):
        return pl.ds(h * HALF, HALF)

    in_txt.wait()
    y_unit, inv_y = unit_rows(txt[...])
    yo[...] = y_unit

    @pl.when(own)
    def _():
        ys[trow(0), :] = y_unit

    in_img.wait()
    for b in range(2):
        rows = pl.ds(b * (BLOCK // 2), BLOCK // 2)
        xo[rows, :] = unit_rows(img[rows, :])[0]

    pl.semaphore_wait(barrier, len(partners))

    def ext(h, dy):
        i = dy if h == 0 else NY
        return rcopy(ys.at[trow(dy), cols(h)], ys.at[trow(dy), cols(h)], e_ss.at[i], e_rs.at[i], at_z(zq))

    def steps(h, right):
        return NY // 2 if right == (h == 0) else NY // 2 - 1

    def ag(h, right, s):
        if right:
            src, dst, to = (NY - (s - 1)) % NY, NY - s, at_y(1)
        else:
            src, dst, to = s - 1, s, at_y(NY - 1)
        i = h * 8 + (0 if right else 4) + s - 1
        return rcopy(ys.at[trow(src), cols(h)], ys.at[trow(dst), cols(h)], ag_ss.at[i], ag_rs.at[i], to)

    @pl.when(own)
    def _():
        ext(1, 0).start()
        for h in range(2):
            for right in (True, False):
                ag(h, right, 1).start()
        ext(0, 0).start()

    QUART = BLOCK // 4
    hx = lax.rem(x, 2)

    def quarter(half, q):
        return pl.ds(pl.multiple_of(half * (BLOCK // 2) + q * QUART, 8), QUART)

    def img_z(q):
        return rcopy(xo.at[quarter(hx, q), :], xs.at[1, quarter(hx, q), :], iz_ss.at[q], iz_rs.at[q], at_z(zp))

    def img_x(q):
        rows = quarter(hx, q)
        to = at_x(1) if q == 0 else at_x(NX - 1)
        return rcopy(xs.at[1, rows, :], xs.at[1, rows, :], ix_ss.at[q], ix_rs.at[q], to)

    def img_core(i):
        if i == 0:
            return rcopy(xo, xs.at[0], ic_ss.at[0], ic_rs.at[0], other)
        rows = quarter(hx, i - 1) if i < 3 else quarter(1 - hx, i - 3)
        return rcopy(xs.at[1, rows, :], xs.at[2, rows, :], ic_ss.at[i], ic_rs.at[i], other)

    for q in range(2):
        img_z(q).start()
    img_core(0).start()

    def put_image(j, block):
        for b in range(2):
            rows = slice(b * (BLOCK // 2), (b + 1) * (BLOCK // 2))
            hi, lo = split_bf16(block[rows, :])
            to = slice(j * BLOCK + b * (BLOCK // 2), j * BLOCK + (b + 1) * (BLOCK // 2))
            xb_hi[to, :] = hi
            xb_lo[to, :] = lo

    def put_text(c):
        rows = slice(c * 2 * TEXT, (c + 1) * 2 * TEXT)
        hi, lo = split_bf16(ys[rows, :])
        yb_hi[rows, :] = hi
        yb_lo[rows, :] = lo

    put_image(0, xo)

    @pl.when(guest)
    def _():
        ext(1, 0).wait_recv()
        for right in (True, False):
            ag(1, right, 1).start()

    scale = jnp.exp(jnp.full((1, 2 * BLOCK), lt_ref[0], F32))
    offset = bias_ref[0]
    lacc[...] = jnp.zeros_like(lacc)

    def pairs(t, half):
        rows = slice(t * TT, (t + 1) * TT)
        at = slice(half * 2 * BLOCK, (half + 1) * 2 * BLOCK)
        prod = dot3(yb_hi[rows, :], yb_lo[rows, :], xb_hi[at, :], xb_lo[at, :], 1, 1)
        logits = scale * prod + offset
        u = jnp.exp(-jnp.abs(logits))
        w = 1.0 + u
        r = 1.0 / w
        sp = jnp.maximum(logits, 0.0) + (jnp.log(w) + (u - (w - 1.0)) * r)
        sig = jnp.where(logits >= 0.0, r, u * r)
        lacc[...] += jnp.sum(sp.reshape(TT // 8, 8, 2 * BLOCK), axis=0)
        hi, lo = split_bf16(sig)
        d_hi[rows, at] = hi
        d_lo[rows, at] = lo

    def text_sums(t):
        rows = slice(t * TT, (t + 1) * TT)
        gy[rows, :] = dot3(d_hi[rows, :], d_lo[rows, :], xb_hi[...], xb_lo[...], 1, 0)

    def ag_step(s):
        @pl.when(own)
        def _():
            for right in (True, False):
                if s <= steps(0, right):
                    ag(0, right, s).wait_recv()
                    if s < steps(0, right):
                        ag(0, right, s + 1).start()
                    ext(0, NY - s if right else s).start()

        for right in (True, False):
            if s <= steps(1, right):
                ag(1, right, s).wait_recv()
                if s < steps(1, right):
                    ag(1, right, s + 1).start()

    def ext_done(*units):
        @pl.when(guest)
        def _():
            for dy in units:
                ext(0, dy).wait_recv()

    ag_step(1)
    img_z(0).wait_recv()
    img_x(0).start()
    img_core(1).start()
    img_core(0).wait_recv()
    put_image(1, xs.at[0])
    ag_step(2)
    img_z(1).wait_recv()
    img_x(1).start()
    img_core(2).start()
    ext_done(1, 7)
    put_text(0)
    img_x(0).wait_recv()
    img_core(3).start()
    ag_step(3)
    ext_done(2, 6)
    put_text(1)
    pairs(0, 0)
    img_x(1).wait_recv()
    img_core(4).start()
    ag_step(4)
    put_image(2, xs.at[1])
    ext_done(3, 5)
    put_text(2)
    for i in range(1, 5):
        img_core(i).wait_recv()
    put_image(3, xs.at[2])
    pairs(0, 1)
    ext_done(0, 4)
    put_text(3)
    pairs(1, 0)
    pairs(1, 1)
    text_sums(1)

    def rs_unit(h, right, s):
        dist = steps(h, right) - s + 1
        return dist if right or dist == 0 else NY - dist

    def rs(h, right, s):
        i = h * 8 + (0 if right else 4) + s - 1
        to = at_y(1 if right else NY - 1)
        return rcopy(gy.at[trow(rs_unit(h, right, s)), cols(h)], rs_in.at[i], rs_ss.at[i], rs_rs.at[i], to)

    def add(dy, h, value):
        at = slice(SLOT[dy] * TEXT, (SLOT[dy] + 1) * TEXT), slice(h * HALF, (h + 1) * HALF)
        gy[at] = gy[at] + value

    def gext(dy):
        return rcopy(gy.at[trow(dy), cols(0)], ge_in.at[dy], ge_ss.at[dy], ge_rs.at[dy], at_z(zq))

    def gfin():
        return rcopy(gy.at[trow(0), cols(1)], gf_in, ge_ss.at[NY], ge_rs.at[NY], at_z(zq))

    def gext_add(dy):
        gext(dy).wait_recv()
        add(dy, 0, ge_in[dy])

    def rs_start(h, s):
        for right in (True, False):
            if s <= steps(h, right):
                rs(h, right, s).start()

    def rs_take(h, s):
        for right in (True, False):
            if s <= steps(h, right):
                rs(h, right, s).wait_recv()
                i = h * 8 + (0 if right else 4) + s - 1
                add(rs_unit(h, right, s + 1), h, rs_in[i])

    @pl.when(guest)
    def _():
        for dy in (4, 3, 5, 0):
            gext(dy).start()

    rs_start(1, 1)
    text_sums(0)

    @pl.when(guest)
    def _():
        for dy in (2, 6, 1, 7):
            gext(dy).start()

    @pl.when(own)
    def _():
        for dy in (4, 5):
            gext_add(dy)
        rs_start(0, 1)

    def gcopy(c):
        return rcopy(gxs.at[c, 1], gc_in.at[c], gc_ss.at[c], gc_rs.at[c], other)

    def image_sums(c):
        at = slice(c * CC, (c + 1) * CC)
        for b in range(2):
            rows = slice(b * 2 * BLOCK, (b + 1) * 2 * BLOCK)
            g = dot3(d_hi[:, rows], d_lo[:, rows], yb_hi[:, at], yb_lo[:, at], 0, 0)
            gxs[c, 0, b] = g[0:BLOCK, :]
            gxs[c, 1, b] = g[BLOCK : 2 * BLOCK, :]
        gcopy(c).start()

    def xrows(d):
        return pl.ds(pl.multiple_of(lax.rem(x + d, NX) * TEXT, 8), TEXT)

    def xa(c, right):
        part = pl.ds(0 if right else CC // 2, CC // 2)
        i = c * 2 + (0 if right else 1)
        src = gxs.at[c, 0, :, xrows(2), part]
        return rcopy(src, xa_in.at[i], xa_ss.at[i], xa_rs.at[i], at_x(1 if right else NX - 1))

    def xf(c, right):
        d = 1 if right else NX - 1
        i = c * 2 + (0 if right else 1)
        return rcopy(gxs.at[c, 0, :, xrows(d), :], xf_in.at[i], xf_ss.at[i], xf_rs.at[i], at_x(d))

    def core_done(c):
        gcopy(c).wait()
        for b in range(2):
            gxs[c, 0, b] = gxs[c, 0, b] + gc_in[c, b]
        for right in (True, False):
            xa(c, right).start()

    def xa_done(c):
        for right in (True, False):
            xa(c, right).wait()
            d = 1 if right else NX - 1
            part = pl.ds(0 if right else CC // 2, CC // 2)
            i = c * 2 + (0 if right else 1)
            for b in range(2):
                gxs[c, 0, b, xrows(d), part] = gxs[c, 0, b, xrows(d), part] + xa_in[i, b]
            xf(c, right).start()

    def q(c, i):
        b, h = (0, 1 - zh) if i == 0 else (1, zh if i == 1 else 1 - zh)
        to = at_z(z + NL) if i == 0 else at_z(zp if i == 1 else zp + NL)
        j = c * 3 + i
        return rcopy(zs.at[c, b, h], zr.at[c, i], q_ss.at[j], q_rs.at[j], to)

    def xf_done(c):
        for right in (True, False):
            xf(c, right).wait()
        for b in range(2):
            v = gxs[c, 0, b, xrows(0), :] + xf_in[c * 2, b] + xf_in[c * 2 + 1, b]
            zs[c, b, 0] = v[0:SHARE, :]
            zs[c, b, 1] = v[SHARE:TEXT, :]
        for i in range(3):
            q(c, i).start()

    image_sums(0)
    image_sums(1)
    image_sums(2)
    core_done(0)

    x_both = xo[xrows(0), :]
    x_own = jnp.where(zh == 0, x_both[0:SHARE, :], x_both[SHARE:TEXT, :])
    y_both = yo[...]
    y_own = jnp.where(zh == 0, y_both[0:SHARE, :], y_both[SHARE:TEXT, :])
    iy_own = jnp.where(zh == 0, inv_y[0:SHARE, :], inv_y[SHARE:TEXT, :])
    scale1 = scale[:, 0:1]
    same = jnp.sum(jnp.sum(x_own * y_own, axis=-1, keepdims=True) * scale1 + offset)
    lc[k] = jnp.full((8, 128), jnp.sum(lacc[...]) - same, F32)

    def lsend(buf, me, ss, rs, to, n):
        copies = [rcopy(buf.at[me], buf.at[me], ss.at[d - 1], rs.at[d - 1], to(d)) for d in range(1, n)]
        for c in copies:
            c.start()
        return copies

    def lsum(buf, copies, n):
        for c in copies:
            c.wait()
        out = buf[0]
        for i in range(1, n):
            out = out + buf[i]
        return out

    def rs_step(s):
        rs_take(1, s)
        rs_start(1, s + 1)

        @pl.when(own)
        def _():
            for dy in ((3, 6), (2, 7), (1,), (0,))[s - 1]:
                gext_add(dy)
            rs_take(0, s)
            rs_start(0, s + 1)

    lcopies = lsend(lc, k, lc_ss, lc_rs, lambda d: other, 2)
    core_done(1)
    rs_step(1)
    core_done(2)
    lx[x] = lsum(lc, lcopies, 2)
    lcopies = lsend(lx, x, lx_ss, lx_rs, at_x, NX)
    xa_done(0)
    rs_step(2)
    xa_done(1)
    xa_done(2)
    ly[y] = lsum(lx, lcopies, NX)
    lcopies = lsend(ly, y, ly_ss, ly_rs, at_y, NY)
    xf_done(0)
    rs_step(3)
    lz[z] = lsum(ly, lcopies, NY)
    lcopies = lsend(lz, z, lz_ss, lz_rs, lambda d: at_z(z + d), NZ)
    xf_done(1)
    rs_step(4)

    @pl.when(guest)
    def _():
        gfin().start()

    hcopy = rcopy(gz.at[1 - zh], gz_in, h_ss, h_rs, at_z(z + NL))

    @pl.when(own)
    def _():
        gfin().wait_recv()
        add(0, 1, gf_in[...])
        gz[0] = gy[SLOT[0] * TEXT : SLOT[0] * TEXT + SHARE, :]
        gz[1] = gy[SLOT[0] * TEXT + SHARE : (SLOT[0] + 1) * TEXT, :]
        hcopy.start()

    xf_done(2)
    loss = lsum(lz, lcopies, NZ) * (1.0 / (float(N) * float(N)))
    loss_o[0] = loss[0, 0]

    for c in range(NC):
        for i in range(3):
            q(c, i).wait()
        gx[:, c * CC : (c + 1) * CC] = zs[c, 0, zh] + zr[c, 0] + zr[c, 1] + zr[c, 2]
    raw = img[xrows(0), :]
    inv_x = unit_rows(jnp.where(zh == 0, raw[0:SHARE, :], raw[SHARE:TEXT, :]))[1]
    g = scale1 * (gx[...] - y_own)
    gi_o[...] = inv_x * (g - x_own * jnp.sum(x_own * g, axis=-1, keepdims=True))

    @pl.when(own)
    def _():
        gt[...] = gz[zh]

    @pl.when(guest)
    def _():
        hcopy.wait_recv()
        gt[...] = gz_in[...]

    g = scale1 * (gt[...] - x_own)
    gt_o[...] = iy_own * (g - y_own * jnp.sum(y_own * g, axis=-1, keepdims=True))

    for i in range(2):
        img_z(i).wait_send()
        img_x(i).wait_send()
    for i in range(5):
        img_core(i).wait_send()
    for right in (True, False):
        for s in range(1, steps(1, right) + 1):
            ag(1, right, s).wait_send()
            rs(1, right, s).wait_send()

    @pl.when(own)
    def _():
        ext(1, 0).wait_send()
        for dy in range(NY):
            ext(0, dy).wait_send()
        for right in (True, False):
            for s in range(1, steps(0, right) + 1):
                ag(0, right, s).wait_send()
                rs(0, right, s).wait_send()
        hcopy.wait_send()

    @pl.when(guest)
    def _():
        for dy in range(NY):
            gext(dy).wait_send()
        gfin().wait_send()


def local(image, text, log_temp, bias):
    vmem = pl.BlockSpec(memory_space=pltpu.VMEM)
    smem = pl.BlockSpec(memory_space=pltpu.SMEM)
    hbm = pl.BlockSpec(memory_space=pl.ANY)
    dma = pltpu.SemaphoreType.DMA
    scratch = [
        pltpu.VMEM((BLOCK, D), F32),
        pltpu.VMEM((TEXT, D), F32),
        pltpu.VMEM((BLOCK, D), F32),
        pltpu.VMEM((TEXT, D), F32),
        pltpu.VMEM((3, BLOCK, D), F32),
        pltpu.VMEM((T, D), F32),
        pltpu.VMEM((S, D), BF16),
        pltpu.VMEM((S, D), BF16),
        pltpu.VMEM((T, D), BF16),
        pltpu.VMEM((T, D), BF16),
        pltpu.VMEM((T, S), BF16),
        pltpu.VMEM((T, S), BF16),
        pltpu.VMEM((T, D), F32),
        pltpu.VMEM((NY, TEXT, HALF), F32),
        pltpu.VMEM((TEXT, HALF), F32),
        pltpu.VMEM((16, TEXT, HALF), F32),
        pltpu.VMEM((2, SHARE, D), F32),
        pltpu.VMEM((SHARE, D), F32),
        pltpu.VMEM((SHARE, D), F32),
        pltpu.VMEM((NC, 2, 2, BLOCK, CC), F32),
        pltpu.VMEM((NC, 2, BLOCK, CC), F32),
        pltpu.VMEM((2 * NC, 2, TEXT, CC // 2), F32),
        pltpu.VMEM((2 * NC, 2, TEXT, CC), F32),
        pltpu.VMEM((NC, 2, 2, SHARE, CC), F32),
        pltpu.VMEM((NC, 3, SHARE, CC), F32),
        pltpu.VMEM((SHARE, D), F32),
        pltpu.VMEM((8, 2 * BLOCK), F32),
        pltpu.VMEM((2, 8, 128), F32),
        pltpu.VMEM((NX, 8, 128), F32),
        pltpu.VMEM((NY, 8, 128), F32),
        pltpu.VMEM((NZ, 8, 128), F32),
        dma((2,)),
    ]
    for n in (NY + 1, 16, 5, 2, 2, NY + 1, 16, NC, 2 * NC, 2 * NC, 3 * NC):
        scratch += [dma((n,)), dma((n,))]
    scratch += [dma, dma]
    for n in (1, NX - 1, NY - 1, NZ - 1):
        scratch += [dma((n,)), dma((n,))]
    loss, gi, gt = pl.pallas_call(
        kernel,
        out_shape=(
            jax.ShapeDtypeStruct((1,), F32),
            jax.ShapeDtypeStruct((SHARE, D), F32),
            jax.ShapeDtypeStruct((SHARE, D), F32),
        ),
        in_specs=[hbm, hbm, smem, smem],
        out_specs=(smem, vmem, vmem),
        scratch_shapes=scratch,
        compiler_params=pltpu.CompilerParams(
            collective_id=0, has_side_effects=True, vmem_limit_bytes=56 << 20
        ),
    )(image, text, log_temp, bias)
    return loss[0], gi, gt


def solution(mesh):
    in_specs = (P("dp", None), P("dp", None), P(), P())
    out_specs = (P(), P(("dp", "split"), None), P(("dp", "split"), None))
    return jax.shard_map(local, mesh=mesh, in_specs=in_specs, out_specs=out_specs, check_vma=False)
```

time: 1200 us -> 83.6 us (0.07)
  the two profiles are of different devices: /device:TPU:2 before, /device:TPU:9 now
where the time goes in v2:
time: 83.6 us; the launch traced here: 83.4 us
  Pallas kernels  77.5 us (93%)
  between operations  3.63 us (4%)
  local copies, waits for them, and re-layouts  2.22 us (3%)
    pallas_call x1, Pallas kernels, local(): pl.pallas_call(kernel, out_shape=(jax.ShapeDtypeStruct((1,), F32), jax.Sh...  77.5 us
    unnamed x4, local copies, waits for them, and re-layouts  2.22 us

profile of v2, /device:TPU:9, one launch (start us, length us, event | category | flops | bytes accessed | tf_op | source)
XLA Modules:
  0.0 83.4 jit_solution(5973992178602337545)
XLA Ops:
  1.9 77.5 %shard_map.67 = (f32[1]{0:T(128)}, f32[28,768]{1,0:T(8,128)}, f32[28,768]{1,0:T(8,128)}) custom-call(f32[224,768]{1,0:T(8,128)} %img_hbm.1, f32[224,768]{1,0:T(8,128)} %txt_hbm.1, f32[1]{0:T(128)S(6)} %copy.10.lt_ref, f32[1]{0:T(128)S(6)} %copy.11.bias_ref), custom_call_target="tpu_custom_call" | custom-call | tf_op jit(solution)/shard_map/pallas_call | solution.py:547
  80.0 0.0 copy-start
  80.0 1.6 %copy.13 = f32[28,768]{1,0:T(8,128)} copy(f32[28,768]{1,0:T(8,128)} %get-tuple-element.13) | data formatting | bytes 172032
  81.6 0.0 copy-done
  81.6 0.6 copy.14
Async XLA Ops:
  80.0 1.6 %copy-start = (f32[28,768]{1,0:T(8,128)S(1)}, f32[28,768]{1,0:T(8,128)}, u32[]{:S(2)}) copy-start(f32[28,768]{1,0:T(8,128)} %get-tuple-element.14) | copy-start | bytes 258052

commit v3 on v0

v3 whole, which is shorter than its diff:
```python
import jax
import jax.numpy as jnp
from jax import lax
from jax.experimental import pallas as pl
from jax.experimental.pallas import tpu as pltpu
from jax.sharding import PartitionSpec as P

EPS = 1e-06
MESH = pl.DeviceIdType.MESH
D = 768
NX, NY, NZ, NL = 4, 8, 8, 4
N = 14336
SHARE = 28
BLOCK = 224
TEXT = 56
GROUP = NX * SHARE
S = 2 * NL * GROUP
ORDER = (0, 1, 3, 2)
T = NY * TEXT
HALF = D // 2
NC = 3
CC = D // NC
LANES = 6
LW = D // LANES
TT = T // 2
F32 = jnp.float32
BF16 = jnp.bfloat16
SLOT = {1: 0, 7: 1, 2: 2, 6: 3, 3: 4, 5: 5, 0: 6, 4: 7}


def split_bf16(v):
    hi = v.astype(BF16)
    return hi, (v - hi.astype(F32)).astype(BF16)


def dot3(ah, al, bh, bl, ca, cb):
    def one(a, b):
        return lax.dot_general(a, b, (((ca,), (cb,)), ((), ())), preferred_element_type=F32)

    return one(ah, bh) + one(al, bh) + one(ah, bl)


def unit_rows(v):
    inv = lax.rsqrt(jnp.sum(v * v, axis=-1, keepdims=True) + EPS)
    return v * inv, inv


def kernel(
    img_hbm, txt_hbm, lt_ref, bias_ref,
    loss_o, gi_o, gt_o,
    img, txt, xh, invx, xo, yo, xs, xc, ys, xb_hi, xb_lo, yb_hi, yb_lo, d_hi, d_lo,
    gy, rs_in, gz, gz_in, gxs, gc_in, xa_in, xf_in, zs, zr, gx, lacc, lc, lx, ly, lz,
    in_s, ag_ss, ag_rs, ic_ss, ic_rs, iz_ss, iz_rs, ix_ss, ix_rs,
    rs_ss, rs_rs, gc_ss, gc_rs, xa_ss, xa_rs, xf_ss, xf_rs, q_ss, q_rs, h_ss, h_rs,
    lc_ss, lc_rs, lx_ss, lx_rs, ly_ss, ly_rs, lz_ss, lz_rs,
):
    dp = lax.axis_index("dp")
    split = lax.axis_index("split")
    k = lax.rem(dp, 2)
    y = lax.rem(lax.div(dp, 2), NY)
    zl = lax.div(dp, 2 * NY)
    x = lax.div(split, 2)
    zh = lax.rem(split, 2)
    z = zh * NL + zl
    def dev(x_, y_, z_, k_):
        return (lax.rem(z_, NL) * (2 * NY) + y_ * 2 + k_, x_ * 2 + lax.div(z_, NL))

    def at_x(d):
        return dev(lax.rem(x + d, NX), y, z, k)

    def at_y(d):
        return dev(x, lax.rem(y + d, NY), z, k)

    def at_z(z_):
        return dev(x, y, lax.rem(z_, NZ), k)

    def at_line(r):
        return dev(x, y, zh * NL + lax.rem(zl + r, NL), k)

    other = dev(x, y, z, 1 - k)

    def rcopy(src, dst, ss, rs, to):
        return pltpu.make_async_remote_copy(src, dst, ss, rs, device_id=to, device_id_type=MESH)

    own_rows = pl.ds(pl.multiple_of(x * TEXT, 8), TEXT)
    in_img = pltpu.make_async_copy(img_hbm, img, in_s.at[0])
    in_txt = pltpu.make_async_copy(txt_hbm.at[own_rows, :], txt, in_s.at[1])
    in_txt.start()
    in_img.start()
    barrier = pltpu.get_barrier_semaphore()
    partners = [at_x(d) for d in range(1, NX)] + [at_y(d) for d in range(1, NY)]
    partners += [at_z(z + d) for d in range(1, NZ)] + [other]
    for to in partners:
        pl.semaphore_signal(barrier, inc=1, device_id=to, device_id_type=MESH)

    def trow(dy):
        return pl.ds(SLOT[dy] * TEXT, TEXT)

    in_txt.wait()
    y_unit, inv_y = unit_rows(txt[...])
    yo[...] = y_unit
    ys[trow(0), :] = y_unit
    in_img.wait()
    for i in range(2 * NX):
        unit, inv = unit_rows(img[i * SHARE : (i + 1) * SHARE, :])
        xh[i % 2, i // 2] = unit
        invx[i % 2, i // 2] = jnp.broadcast_to(inv, (SHARE, 128))
        xo[i % 2, i // 2 * SHARE : (i // 2 + 1) * SHARE, :] = unit

    pl.semaphore_wait(barrier, len(partners))

    def lane_cols(n):
        return pl.ds(n * LW, LW)

    def steps(n, right):
        return NY // 2 if right == (n % 2 == 0) else NY // 2 - 1

    def ag(n, right, s):
        if right:
            src, dst, to = (NY - (s - 1)) % NY, NY - s, at_y(1)
        else:
            src, dst, to = s - 1, s, at_y(NY - 1)
        i = n * 8 + (0 if right else 4) + s - 1
        return rcopy(ys.at[trow(src), lane_cols(n)], ys.at[trow(dst), lane_cols(n)], ag_ss.at[i], ag_rs.at[i], to)

    for n in range(LANES):
        for right in (True, False):
            ag(n, right, 1).start()

    hx = lax.rem(x, 2)

    def half(h):
        return pl.ds(pl.multiple_of(h * HALF, 128), HALF)

    def img_z(r):
        z_ = z + {1: NZ - 1, 3: 1}[r] if r != 2 else z + 2 + NL * k
        there = lax.div(lax.rem(z_, NZ), NL)
        return rcopy(xo.at[there, :, half(hx)], xs.at[r - 1, :, half(hx)], iz_ss.at[r - 1], iz_rs.at[r - 1], at_z(z_))

    def img_x(r, right):
        i = (r - 1) * 2 + (0 if right else 1)
        ref = xs.at[r - 1, pl.ds(0 if right else GROUP // 2, GROUP // 2), half(hx)]
        return rcopy(ref, ref, ix_ss.at[i], ix_rs.at[i], at_x(1 if right else NX - 1))

    def core_z(r):
        return rcopy(xs.at[r - 1, :, half(hx)], xc.at[r, :, half(hx)], ic_ss.at[r], ic_rs.at[r], other)

    def core_x(r, right):
        i = NL + (r - 1) * 2 + (0 if right else 1)
        rows = pl.ds(0 if right else GROUP // 2, GROUP // 2)
        src = xs.at[r - 1, rows, half(1 - hx)]
        return rcopy(src, xc.at[r, rows, half(1 - hx)], ic_ss.at[i], ic_rs.at[i], other)

    core_own = rcopy(xo.at[zh], xc.at[0], ic_ss.at[0], ic_rs.at[0], other)
    for r in (1, 3, 2):
        img_z(r).start()
    core_own.start()

    def from_z(r):
        img_z(r).wait_recv()
        for right in (True, False):
            img_x(r, right).start()
        core_z(r).start()

    def from_x(r):
        for right in (True, False):
            img_x(r, right).wait_recv()
            core_x(r, right).start()

    def from_core(r):
        core_z(r).wait_recv()
        for right in (True, False):
            core_x(r, right).wait_recv()

    def put_image(r, block, kk):
        g = ORDER.index(r) * 2 + kk
        rows = slice(g * GROUP, (g + 1) * GROUP)
        hi, lo = split_bf16(block)
        xb_hi[rows, :] = hi
        xb_lo[rows, :] = lo

    def put_text(c):
        rows = slice(c * 2 * TEXT, (c + 1) * 2 * TEXT)
        hi, lo = split_bf16(ys[rows, :])
        yb_hi[rows, :] = hi
        yb_lo[rows, :] = lo

    put_image(0, xo[zh], 0)

    scale = jnp.exp(jnp.full((1, S // 2), lt_ref[0], F32))
    offset = bias_ref[0]
    lacc[...] = jnp.zeros_like(lacc)

    def pairs(t, half):
        rows = slice(t * TT, (t + 1) * TT)
        at = slice(half * S // 2, (half + 1) * S // 2)
        prod = dot3(yb_hi[rows, :], yb_lo[rows, :], xb_hi[at, :], xb_lo[at, :], 1, 1)
        logits = scale * prod + offset
        u = jnp.exp(-jnp.abs(logits))
        w = 1.0 + u
        r = 1.0 / w
        sp = jnp.maximum(logits, 0.0) + (jnp.log(w) + (u - (w - 1.0)) * r)
        sig = jnp.where(logits >= 0.0, r, u * r)
        lacc[...] += jnp.sum(sp.reshape(TT // 8, 8, S // 2), axis=0)
        hi, lo = split_bf16(sig)
        d_hi[rows, at] = hi
        d_lo[rows, at] = lo

    def text_sums(t):
        rows = slice(t * TT, (t + 1) * TT)
        gy[rows, :] = dot3(d_hi[rows, :], d_lo[rows, :], xb_hi[...], xb_lo[...], 1, 0)

    def ag_take(s):
        for n in range(LANES):
            for right in (True, False):
                if s <= steps(n, right):
                    ag(n, right, s).wait_recv()
                    if s < steps(n, right):
                        ag(n, right, s + 1).start()

    ag_take(1)
    core_own.wait_recv()
    put_image(0, xc[0], 1)
    put_text(0)
    from_z(1)
    from_z(3)
    ag_take(2)
    put_text(1)
    ag_take(3)
    put_text(2)
    from_z(2)
    from_x(1)
    put_image(1, xs[0], 0)
    from_x(3)
    put_image(3, xs[2], 0)
    ag_take(4)
    put_text(3)
    from_core(1)
    put_image(1, xc[1], 1)
    pairs(1, 0)
    from_x(2)
    put_image(2, xs[1], 0)
    pairs(0, 0)
    from_core(3)
    put_image(3, xc[3], 1)
    from_core(2)
    put_image(2, xc[2], 1)
    pairs(1, 1)
    pairs(0, 1)

    x_own = xh[zh, x]
    y_both = yo[...]
    y_own = jnp.where(zh == 0, y_both[0:SHARE, :], y_both[SHARE:TEXT, :])
    iy_own = jnp.where(zh == 0, inv_y[0:SHARE, :], inv_y[SHARE:TEXT, :])
    scale1 = scale[:, 0:1]
    same = jnp.sum(jnp.sum(x_own * y_own, axis=-1, keepdims=True) * scale1 + offset)
    lc[k] = jnp.full((8, 128), jnp.sum(lacc[...]) - same, F32)

    def lsend(buf, me, ss, rs, to, n):
        copies = [rcopy(buf.at[me], buf.at[me], ss.at[d - 1], rs.at[d - 1], to(d)) for d in range(1, n)]
        for c in copies:
            c.start()
        return copies

    def lsum(buf, copies, n):
        for c in copies:
            c.wait()
        out = buf[0]
        for i in range(1, n):
            out = out + buf[i]
        return out

    lcopies = lsend(lc, k, lc_ss, lc_rs, lambda d: other, 2)

    def rs_unit(n, right, s):
        dist = steps(n, right) - s + 1
        return dist if right or dist == 0 else NY - dist

    def rs(n, right, s):
        i = n * 8 + (0 if right else 4) + s - 1
        to = at_y(1 if right else NY - 1)
        src = gy.at[trow(rs_unit(n, right, s)), lane_cols(n)]
        return rcopy(src, rs_in.at[i], rs_ss.at[i], rs_rs.at[i], to)

    def rs_start():
        for n in range(LANES):
            for right in (True, False):
                rs(n, right, 1).start()

    def rs_take(s):
        for n in range(LANES):
            for right in (True, False):
                if s <= steps(n, right):
                    rs(n, right, s).wait_recv()
                    i = n * 8 + (0 if right else 4) + s - 1
                    unit = rs_unit(n, right, s + 1)
                    at = slice(SLOT[unit] * TEXT, (SLOT[unit] + 1) * TEXT), slice(n * LW, (n + 1) * LW)
                    gy[at] = gy[at] + rs_in[i]
                    if s < steps(n, right):
                        rs(n, right, s + 1).start()

    def gcopy(c):
        return rcopy(gxs.at[c, 1], gc_in.at[c], gc_ss.at[c], gc_rs.at[c], other)

    def image_sums(c):
        at = slice(c * CC, (c + 1) * CC)
        for b in range(2):
            rows = slice(b * S // 2, (b + 1) * S // 2)
            g = dot3(d_hi[:, rows], d_lo[:, rows], yb_hi[:, at], yb_lo[:, at], 0, 0)
            for i in range(NL):
                r = ORDER[b * 2 + i // 2]
                for j in range(NX):
                    gxs[c, i % 2, j, r] = g[i * GROUP + j * SHARE : i * GROUP + (j + 1) * SHARE, :]
        gcopy(c).start()

    def ahead(d):
        return lax.rem(x + d, NX)

    def xa(c, right):
        b = 0 if right else 1
        i = c * 2 + b
        src = gxs.at[c, 0, ahead(2), pl.ds(b * 2, 2)]
        return rcopy(src, xa_in.at[i], xa_ss.at[i], xa_rs.at[i], at_x(1 if right else NX - 1))

    def xf(c, right):
        d = 1 if right else NX - 1
        i = c * 2 + (0 if right else 1)
        return rcopy(gxs.at[c, 0, ahead(d)], xf_in.at[i], xf_ss.at[i], xf_rs.at[i], at_x(d))

    def core_done(c):
        gcopy(c).wait()
        for j in range(NX):
            gxs[c, 0, j] = gxs[c, 0, j] + gc_in[c, j]
        for right in (True, False):
            xa(c, right).start()

    def xa_done(c):
        for right in (True, False):
            xa(c, right).wait()
            d = 1 if right else NX - 1
            b = 0 if right else 1
            for i in range(2):
                r = b * 2 + i
                gxs[c, 0, ahead(d), r] = gxs[c, 0, ahead(d), r] + xa_in[c * 2 + b, i]
            xf(c, right).start()

    def q(c, r):
        i = c * 3 + r - 1
        return rcopy(zs.at[c, r], zr.at[c, r - 1], q_ss.at[i], q_rs.at[i], at_line(r))

    def xf_done(c):
        for right in (True, False):
            xf(c, right).wait()
        zs[c] = gxs[c, 0, x] + xf_in[c * 2] + xf_in[c * 2 + 1]
        for r in (2, 1, 3):
            q(c, r).start()

    image_sums(0)
    text_sums(1)
    rs_start()
    core_done(0)
    text_sums(0)
    image_sums(1)
    lx[x] = lsum(lc, lcopies, 2)
    lcopies = lsend(lx, x, lx_ss, lx_rs, at_x, NX)
    core_done(1)
    rs_take(1)
    image_sums(2)
    xa_done(0)
    core_done(2)
    xa_done(1)
    ly[y] = lsum(lx, lcopies, NX)
    lcopies = lsend(ly, y, ly_ss, ly_rs, at_y, NY)
    rs_take(2)
    xf_done(0)
    xa_done(2)
    rs_take(3)
    xf_done(1)
    lz[z] = lsum(ly, lcopies, NY)
    lcopies = lsend(lz, z, lz_ss, lz_rs, lambda d: at_z(z + d), NZ)
    rs_take(4)
    gz[0] = gy[SLOT[0] * TEXT : SLOT[0] * TEXT + SHARE, :]
    gz[1] = gy[SLOT[0] * TEXT + SHARE : (SLOT[0] + 1) * TEXT, :]
    hcopy = rcopy(gz.at[1 - zh], gz_in, h_ss, h_rs, at_z(z + NL))
    hcopy.start()
    xf_done(2)
    loss = lsum(lz, lcopies, NZ) * (1.0 / (float(N) * float(N)))
    loss_o[0] = loss[0, 0]

    for c in range(NC):
        for r in range(1, NL):
            q(c, r).wait()
        gx[:, c * CC : (c + 1) * CC] = zs[c, 0] + zr[c, 0] + zr[c, 1] + zr[c, 2]
    inv_x = invx[zh, x][:, 0:1]
    g = scale1 * (gx[...] - y_own)
    gi_o[...] = inv_x * (g - x_own * jnp.sum(x_own * g, axis=-1, keepdims=True))

    hcopy.wait()
    g = scale1 * (gz[zh] + gz_in[...] - x_own)
    gt_o[...] = iy_own * (g - y_own * jnp.sum(y_own * g, axis=-1, keepdims=True))

    core_own.wait_send()
    for r in range(1, NL):
        img_z(r).wait_send()
        core_z(r).wait_send()
        for right in (True, False):
            img_x(r, right).wait_send()
            core_x(r, right).wait_send()
    for n in range(LANES):
        for right in (True, False):
            for s in range(1, steps(n, right) + 1):
                ag(n, right, s).wait_send()
                rs(n, right, s).wait_send()


def local(image, text, log_temp, bias):
    vmem = pl.BlockSpec(memory_space=pltpu.VMEM)
    smem = pl.BlockSpec(memory_space=pltpu.SMEM)
    hbm = pl.BlockSpec(memory_space=pl.ANY)
    dma = pltpu.SemaphoreType.DMA
    scratch = [
        pltpu.VMEM((BLOCK, D), F32),
        pltpu.VMEM((TEXT, D), F32),
        pltpu.VMEM((2, NX, SHARE, D), F32),
        pltpu.VMEM((2, NX, SHARE, 128), F32),
        pltpu.VMEM((2, GROUP, D), F32),
        pltpu.VMEM((TEXT, D), F32),
        pltpu.VMEM((NL - 1, GROUP, D), F32),
        pltpu.VMEM((NL, GROUP, D), F32),
        pltpu.VMEM((T, D), F32),
        pltpu.VMEM((S, D), BF16),
        pltpu.VMEM((S, D), BF16),
        pltpu.VMEM((T, D), BF16),
        pltpu.VMEM((T, D), BF16),
        pltpu.VMEM((T, S), BF16),
        pltpu.VMEM((T, S), BF16),
        pltpu.VMEM((T, D), F32),
        pltpu.VMEM((8 * LANES, TEXT, LW), F32),
        pltpu.VMEM((2, SHARE, D), F32),
        pltpu.VMEM((SHARE, D), F32),
        pltpu.VMEM((NC, 2, NX, NL, SHARE, CC), F32),
        pltpu.VMEM((NC, NX, NL, SHARE, CC), F32),
        pltpu.VMEM((2 * NC, 2, SHARE, CC), F32),
        pltpu.VMEM((2 * NC, NL, SHARE, CC), F32),
        pltpu.VMEM((NC, NL, SHARE, CC), F32),
        pltpu.VMEM((NC, NL - 1, SHARE, CC), F32),
        pltpu.VMEM((SHARE, D), F32),
        pltpu.VMEM((8, S // 2), F32),
        pltpu.VMEM((2, 8, 128), F32),
        pltpu.VMEM((NX, 8, 128), F32),
        pltpu.VMEM((NY, 8, 128), F32),
        pltpu.VMEM((NZ, 8, 128), F32),
        dma((2,)),
    ]
    for n in (8 * LANES, 10, 3, 6, 8 * LANES, NC, 2 * NC, 2 * NC, 3 * NC):
        scratch += [dma((n,)), dma((n,))]
    scratch += [dma, dma]
    for n in (1, NX - 1, NY - 1, NZ - 1):
        scratch += [dma((n,)), dma((n,))]
    loss, gi, gt = pl.pallas_call(
        kernel,
        out_shape=(
            jax.ShapeDtypeStruct((1,), F32),
            jax.ShapeDtypeStruct((SHARE, D), F32),
            jax.ShapeDtypeStruct((SHARE, D), F32),
        ),
        in_specs=[hbm, hbm, smem, smem],
        out_specs=(smem, vmem, vmem),
        scratch_shapes=scratch,
        compiler_params=pltpu.CompilerParams(
            collective_id=0, has_side_effects=True, vmem_limit_bytes=56 << 20
        ),
    )(image, text, log_temp, bias)
    return loss[0], gi, gt


def solution(mesh):
    in_specs = (P("dp", None), P("dp", None), P(), P())
    out_specs = (P(), P(("dp", "split"), None), P(("dp", "split"), None))
    return jax.shard_map(local, mesh=mesh, in_specs=in_specs, out_specs=out_specs, check_vma=False)
```

time: 1200 us -> 77.4 us (0.06)
  the two profiles are of different devices: /device:TPU:2 before, /device:TPU:8 now
where the time goes in v3:
time: 77.4 us; the launch traced here: 77.2 us
  Pallas kernels  71.4 us (92%)
  between operations  3.63 us (5%)
  local copies, waits for them, and re-layouts  2.22 us (3%)
    pallas_call x1, Pallas kernels, local(): pl.pallas_call(kernel, out_shape=(jax.ShapeDtypeStruct((1,), F32), jax.Sh...  71.4 us
    unnamed x4, local copies, waits for them, and re-layouts  2.22 us

profile of v3, /device:TPU:8, one launch (start us, length us, event | category | flops | bytes accessed | tf_op | source)
XLA Modules:
  0.0 77.2 jit_solution(10103021914964063224)
XLA Ops:
  1.9 71.4 %shard_map.67 = (f32[1]{0:T(128)}, f32[28,768]{1,0:T(8,128)}, f32[28,768]{1,0:T(8,128)}) custom-call(f32[224,768]{1,0:T(8,128)} %img_hbm.1, f32[224,768]{1,0:T(8,128)} %txt_hbm.1, f32[1]{0:T(128)S(6)} %copy.10.lt_ref, f32[1]{0:T(128)S(6)} %copy.11.bias_ref), custom_call_target="tpu_custom_call" | custom-call | tf_op jit(solution)/shard_map/pallas_call | solution.py:460
  73.9 0.0 copy-start
  73.9 1.6 %copy.13 = f32[28,768]{1,0:T(8,128)} copy(f32[28,768]{1,0:T(8,128)} %get-tuple-element.13) | data formatting | bytes 172032
  75.4 0.0 copy-done
  75.4 0.6 copy.14
Async XLA Ops:
  73.9 1.6 %copy-start = (f32[28,768]{1,0:T(8,128)S(1)}, f32[28,768]{1,0:T(8,128)}, u32[]{:S(2)}) copy-start(f32[28,768]{1,0:T(8,128)} %get-tuple-element.14) | copy-start | bytes 258052

commit v4 on v3

--- a/solution.py
+++ b/solution.py
@@ -20,7 +20,7 @@
 HALF = D // 2
 NC = 3
 CC = D // NC
-LANES = 6
+LANES = 3
 LW = D // LANES
 TT = T // 2
 F32 = jnp.float32
@@ -48,7 +48,7 @@
 def kernel(
     img_hbm, txt_hbm, lt_ref, bias_ref,
     loss_o, gi_o, gt_o,
-    img, txt, xh, invx, xo, yo, xs, xc, ys, xb_hi, xb_lo, yb_hi, yb_lo, d_hi, d_lo,
+    img, txt, xo, yo, xs, xc, ys, xb_hi, xb_lo, yb_hi, yb_lo, d_hi, d_lo,
     gy, rs_in, gz, gz_in, gxs, gc_in, xa_in, xf_in, zs, zr, gx, lacc, lc, lx, ly, lz,
     in_s, ag_ss, ag_rs, ic_ss, ic_rs, iz_ss, iz_rs, ix_ss, ix_rs,
     rs_ss, rs_rs, gc_ss, gc_rs, xa_ss, xa_rs, xf_ss, xf_rs, q_ss, q_rs, h_ss, h_rs,
@@ -100,13 +100,6 @@
     y_unit, inv_y = unit_rows(txt[...])
     yo[...] = y_unit
     ys[trow(0), :] = y_unit
-    in_img.wait()
-    for i in range(2 * NX):
-        unit, inv = unit_rows(img[i * SHARE : (i + 1) * SHARE, :])
-        xh[i % 2, i // 2] = unit
-        invx[i % 2, i // 2] = jnp.broadcast_to(inv, (SHARE, 128))
-        xo[i % 2, i // 2 * SHARE : (i // 2 + 1) * SHARE, :] = unit
-
     pl.semaphore_wait(barrier, len(partners))
 
     def lane_cols(n):
@@ -121,11 +114,16 @@
         else:
             src, dst, to = s - 1, s, at_y(NY - 1)
         i = n * 8 + (0 if right else 4) + s - 1
-        return rcopy(ys.at[trow(src), lane_cols(n)], ys.at[trow(dst), lane_cols(n)], ag_ss.at[i], ag_rs.at[i], to)
+        return rcopy(ys.at[trow(src), lane_cols(n)], ys.at[trow(dst), lane_cols(n)], ag_ss, ag_rs.at[i], to)
 
     for n in range(LANES):
         for right in (True, False):
             ag(n, right, 1).start()
+
+    in_img.wait()
+    unit = unit_rows(img[...])[0]
+    for i in range(2 * NX):
+        xo[i % 2, i // 2 * SHARE : (i // 2 + 1) * SHARE, :] = unit[i * SHARE : (i + 1) * SHARE, :]
 
     hx = lax.rem(x, 2)
 
@@ -157,20 +155,20 @@
     core_own.start()
 
     def from_z(r):
-        img_z(r).wait_recv()
+        img_z(r).wait()
         for right in (True, False):
             img_x(r, right).start()
         core_z(r).start()
 
     def from_x(r):
         for right in (True, False):
-            img_x(r, right).wait_recv()
+            img_x(r, right).wait()
             core_x(r, right).start()
 
     def from_core(r):
-        core_z(r).wait_recv()
-        for right in (True, False):
-            core_x(r, right).wait_recv()
+        core_z(r).wait()
+        for right in (True, False):
+            core_x(r, right).wait()
 
     def put_image(r, block, kk):
         g = ORDER.index(r) * 2 + kk
@@ -219,36 +217,42 @@
                         ag(n, right, s + 1).start()
 
     ag_take(1)
-    core_own.wait_recv()
+    core_own.wait()
     put_image(0, xc[0], 1)
-    put_text(0)
     from_z(1)
     from_z(3)
+    put_text(0)
     ag_take(2)
     put_text(1)
+    from_z(2)
     ag_take(3)
     put_text(2)
-    from_z(2)
     from_x(1)
+    from_x(3)
     put_image(1, xs[0], 0)
-    from_x(3)
     put_image(3, xs[2], 0)
+    from_core(1)
+    put_image(1, xc[1], 1)
+    pairs(0, 0)
+    from_x(2)
+    from_core(3)
+    put_image(3, xc[3], 1)
+    put_image(2, xs[1], 0)
+    from_core(2)
+    put_image(2, xc[2], 1)
+    pairs(0, 1)
     ag_take(4)
     put_text(3)
-    from_core(1)
-    put_image(1, xc[1], 1)
     pairs(1, 0)
-    from_x(2)
-    put_image(2, xs[1], 0)
-    pairs(0, 0)
-    from_core(3)
-    put_image(3, xc[3], 1)
-    from_core(2)
-    put_image(2, xc[2], 1)
     pairs(1, 1)
-    pairs(0, 1)
-
-    x_own = xh[zh, x]
+
+    sent = pl.ds(0, (NY - 1) * TEXT)
+    rcopy(ys.at[sent, :], ys.at[sent, :], ag_ss, ag_rs.at[0], other).wait_send()
+
+    raw = img[0:SHARE, :]
+    for i in range(1, 2 * NX):
+        raw = jnp.where(split == i, img[i * SHARE : (i + 1) * SHARE, :], raw)
+    x_own, inv_x = unit_rows(raw)
     y_both = yo[...]
     y_own = jnp.where(zh == 0, y_both[0:SHARE, :], y_both[SHARE:TEXT, :])
     iy_own = jnp.where(zh == 0, inv_y[0:SHARE, :], inv_y[SHARE:TEXT, :])
@@ -280,7 +284,7 @@
         i = n * 8 + (0 if right else 4) + s - 1
         to = at_y(1 if right else NY - 1)
         src = gy.at[trow(rs_unit(n, right, s)), lane_cols(n)]
-        return rcopy(src, rs_in.at[i], rs_ss.at[i], rs_rs.at[i], to)
+        return rcopy(src, rs_in.at[i], rs_ss, rs_rs.at[i], to)
 
     def rs_start():
         for n in range(LANES):
@@ -356,34 +360,34 @@
             q(c, r).start()
 
     image_sums(0)
+    image_sums(1)
     text_sums(1)
     rs_start()
     core_done(0)
+    image_sums(2)
+    core_done(1)
     text_sums(0)
-    image_sums(1)
     lx[x] = lsum(lc, lcopies, 2)
     lcopies = lsend(lx, x, lx_ss, lx_rs, at_x, NX)
-    core_done(1)
+    core_done(2)
+    xa_done(0)
     rs_take(1)
-    image_sums(2)
-    xa_done(0)
-    core_done(2)
     xa_done(1)
+    xa_done(2)
     ly[y] = lsum(lx, lcopies, NX)
     lcopies = lsend(ly, y, ly_ss, ly_rs, at_y, NY)
     rs_take(2)
     xf_done(0)
-    xa_done(2)
+    xf_done(1)
     rs_take(3)
-    xf_done(1)
     lz[z] = lsum(ly, lcopies, NY)
     lcopies = lsend(lz, z, lz_ss, lz_rs, lambda d: at_z(z + d), NZ)
+    xf_done(2)
     rs_take(4)
     gz[0] = gy[SLOT[0] * TEXT : SLOT[0] * TEXT + SHARE, :]
     gz[1] = gy[SLOT[0] * TEXT + SHARE : (SLOT[0] + 1) * TEXT, :]
     hcopy = rcopy(gz.at[1 - zh], gz_in, h_ss, h_rs, at_z(z + NL))
     hcopy.start()
-    xf_done(2)
     loss = lsum(lz, lcopies, NZ) * (1.0 / (float(N) * float(N)))
     loss_o[0] = loss[0, 0]
 
@@ -391,7 +395,6 @@
         for r in range(1, NL):
             q(c, r).wait()
         gx[:, c * CC : (c + 1) * CC] = zs[c, 0] + zr[c, 0] + zr[c, 1] + zr[c, 2]
-    inv_x = invx[zh, x][:, 0:1]
     g = scale1 * (gx[...] - y_own)
     gi_o[...] = inv_x * (g - x_own * jnp.sum(x_own * g, axis=-1, keepdims=True))
 
@@ -399,18 +402,7 @@
     g = scale1 * (gz[zh] + gz_in[...] - x_own)
     gt_o[...] = iy_own * (g - y_own * jnp.sum(y_own * g, axis=-1, keepdims=True))
 
-    core_own.wait_send()
-    for r in range(1, NL):
-        img_z(r).wait_send()
-        core_z(r).wait_send()
-        for right in (True, False):
-            img_x(r, right).wait_send()
-            core_x(r, right).wait_send()
-    for n in range(LANES):
-        for right in (True, False):
-            for s in range(1, steps(n, right) + 1):
-                ag(n, right, s).wait_send()
-                rs(n, right, s).wait_send()
+    rcopy(gy.at[sent, :], gy.at[sent, :], rs_ss, rs_rs.at[0], other).wait_send()
 
 
 def local(image, text, log_temp, bias):
@@ -421,8 +413,6 @@
     scratch = [
         pltpu.VMEM((BLOCK, D), F32),
         pltpu.VMEM((TEXT, D), F32),
-        pltpu.VMEM((2, NX, SHARE, D), F32),
-        pltpu.VMEM((2, NX, SHARE, 128), F32),
         pltpu.VMEM((2, GROUP, D), F32),
         pltpu.VMEM((TEXT, D), F32),
         pltpu.VMEM((NL - 1, GROUP, D), F32),
@@ -452,7 +442,11 @@
         pltpu.VMEM((NZ, 8, 128), F32),
         dma((2,)),
     ]
-    for n in (8 * LANES, 10, 3, 6, 8 * LANES, NC, 2 * NC, 2 * NC, 3 * NC):
+    scratch += [dma, dma((8 * LANES,))]
+    for n in (10, 3, 6):
+        scratch += [dma((n,)), dma((n,))]
+    scratch += [dma, dma((8 * LANES,))]
+    for n in (NC, 2 * NC, 2 * NC, 3 * NC):
         scratch += [dma((n,)), dma((n,))]
     scratch += [dma, dma]
     for n in (1, NX - 1, NY - 1, NZ - 1):

time: 77.4 us -> 73.4 us (0.948)
  Pallas kernels: 71.4 us -> 67.4 us
    pallas_call x1, Pallas kernels: 71.4 us -> 67.4 us  [local(): pl.pallas_call(kernel, out_shape=(jax.ShapeDtypeStruct((1,), F32), jax.Sh...]
where the time goes in v4:
time: 73.4 us; the launch traced here: 73.2 us
  Pallas kernels  67.4 us (92%)
  between operations  3.63 us (5%)
  local copies, waits for them, and re-layouts  2.22 us (3%)
    pallas_call x1, Pallas kernels, local(): pl.pallas_call(kernel, out_shape=(jax.ShapeDtypeStruct((1,), F32), jax.Sh...  67.4 us
    unnamed x4, local copies, waits for them, and re-layouts  2.22 us

profile of v4, /device:TPU:8, one launch (start us, length us, event | category | flops | bytes accessed | tf_op | source)
XLA Modules:
  0.0 73.2 jit_solution(15069844868396799455)
XLA Ops:
  1.9 67.4 %shard_map.67 = (f32[1]{0:T(128)}, f32[28,768]{1,0:T(8,128)}, f32[28,768]{1,0:T(8,128)}) custom-call(f32[224,768]{1,0:T(8,128)} %img_hbm.1, f32[224,768]{1,0:T(8,128)} %txt_hbm.1, f32[1]{0:T(128)S(6)} %copy.10.lt_ref, f32[1]{0:T(128)S(6)} %copy.11.bias_ref), custom_call_target="tpu_custom_call" | custom-call | tf_op jit(solution)/shard_map/pallas_call | solution.py:454
  69.9 0.0 copy-start
  69.9 1.6 %copy.13 = f32[28,768]{1,0:T(8,128)} copy(f32[28,768]{1,0:T(8,128)} %get-tuple-element.13) | data formatting | bytes 172032
  71.4 0.0 copy-done
  71.4 0.6 copy.14
Async XLA Ops:
  69.9 1.6 %copy-start = (f32[28,768]{1,0:T(8,128)S(1)}, f32[28,768]{1,0:T(8,128)}, u32[]{:S(2)}) copy-start(f32[28,768]{1,0:T(8,128)} %get-tuple-element.14) | copy-start | bytes 258052

commit v5 on v4

--- a/solution.py
+++ b/solution.py
@@ -47,7 +47,7 @@
 
 def kernel(
     img_hbm, txt_hbm, lt_ref, bias_ref,
-    loss_o, gi_o, gt_o,
+    loss_o, g_o,
     img, txt, xo, yo, xs, xc, ys, xb_hi, xb_lo, yb_hi, yb_lo, d_hi, d_lo,
     gy, rs_in, gz, gz_in, gxs, gc_in, xa_in, xf_in, zs, zr, gx, lacc, lc, lx, ly, lz,
     in_s, ag_ss, ag_rs, ic_ss, ic_rs, iz_ss, iz_rs, ix_ss, ix_rs,
@@ -258,7 +258,7 @@
     iy_own = jnp.where(zh == 0, inv_y[0:SHARE, :], inv_y[SHARE:TEXT, :])
     scale1 = scale[:, 0:1]
     same = jnp.sum(jnp.sum(x_own * y_own, axis=-1, keepdims=True) * scale1 + offset)
-    lc[k] = jnp.full((8, 128), jnp.sum(lacc[...]) - same, F32)
+    ly[y] = jnp.full((8, 128), jnp.sum(lacc[...]) - same, F32)
 
     def lsend(buf, me, ss, rs, to, n):
         copies = [rcopy(buf.at[me], buf.at[me], ss.at[d - 1], rs.at[d - 1], to(d)) for d in range(1, n)]
@@ -274,7 +274,7 @@
             out = out + buf[i]
         return out
 
-    lcopies = lsend(lc, k, lc_ss, lc_rs, lambda d: other, 2)
+    lcopies = lsend(ly, y, ly_ss, ly_rs, at_y, NY)
 
     def rs_unit(n, right, s):
         dist = steps(n, right) - s + 1
@@ -367,28 +367,28 @@
     image_sums(2)
     core_done(1)
     text_sums(0)
-    lx[x] = lsum(lc, lcopies, 2)
-    lcopies = lsend(lx, x, lx_ss, lx_rs, at_x, NX)
+    lz[z] = lsum(ly, lcopies, NY)
+    lcopies = lsend(lz, z, lz_ss, lz_rs, lambda d: at_z(z + d), NZ)
     core_done(2)
     xa_done(0)
     rs_take(1)
     xa_done(1)
     xa_done(2)
-    ly[y] = lsum(lx, lcopies, NX)
-    lcopies = lsend(ly, y, ly_ss, ly_rs, at_y, NY)
     rs_take(2)
+    lc[k] = lsum(lz, lcopies, NZ)
+    lcopies = lsend(lc, k, lc_ss, lc_rs, lambda d: other, 2)
     xf_done(0)
+    lx[x] = lsum(lc, lcopies, 2)
+    lcopies = lsend(lx, x, lx_ss, lx_rs, at_x, NX)
     xf_done(1)
     rs_take(3)
-    lz[z] = lsum(ly, lcopies, NY)
-    lcopies = lsend(lz, z, lz_ss, lz_rs, lambda d: at_z(z + d), NZ)
     xf_done(2)
     rs_take(4)
     gz[0] = gy[SLOT[0] * TEXT : SLOT[0] * TEXT + SHARE, :]
     gz[1] = gy[SLOT[0] * TEXT + SHARE : (SLOT[0] + 1) * TEXT, :]
     hcopy = rcopy(gz.at[1 - zh], gz_in, h_ss, h_rs, at_z(z + NL))
     hcopy.start()
-    loss = lsum(lz, lcopies, NZ) * (1.0 / (float(N) * float(N)))
+    loss = lsum(lx, lcopies, NX) * (1.0 / (float(N) * float(N)))
     loss_o[0] = loss[0, 0]
 
     for c in range(NC):
@@ -396,11 +396,11 @@
             q(c, r).wait()
         gx[:, c * CC : (c + 1) * CC] = zs[c, 0] + zr[c, 0] + zr[c, 1] + zr[c, 2]
     g = scale1 * (gx[...] - y_own)
-    gi_o[...] = inv_x * (g - x_own * jnp.sum(x_own * g, axis=-1, keepdims=True))
+    g_o[0] = inv_x * (g - x_own * jnp.sum(x_own * g, axis=-1, keepdims=True))
 
     hcopy.wait()
     g = scale1 * (gz[zh] + gz_in[...] - x_own)
-    gt_o[...] = iy_own * (g - y_own * jnp.sum(y_own * g, axis=-1, keepdims=True))
+    g_o[1] = iy_own * (g - y_own * jnp.sum(y_own * g, axis=-1, keepdims=True))
 
     rcopy(gy.at[sent, :], gy.at[sent, :], rs_ss, rs_rs.at[0], other).wait_send()
 
@@ -451,21 +451,20 @@
     scratch += [dma, dma]
     for n in (1, NX - 1, NY - 1, NZ - 1):
         scratch += [dma((n,)), dma((n,))]
-    loss, gi, gt = pl.pallas_call(
+    loss, g = pl.pallas_call(
         kernel,
         out_shape=(
             jax.ShapeDtypeStruct((1,), F32),
-            jax.ShapeDtypeStruct((SHARE, D), F32),
-            jax.ShapeDtypeStruct((SHARE, D), F32),
+            jax.ShapeDtypeStruct((2, SHARE, D), F32),
         ),
         in_specs=[hbm, hbm, smem, smem],
-        out_specs=(smem, vmem, vmem),
+        out_specs=(smem, vmem),
         scratch_shapes=scratch,
         compiler_params=pltpu.CompilerParams(
             collective_id=0, has_side_effects=True, vmem_limit_bytes=56 << 20
         ),
     )(image, text, log_temp, bias)
-    return loss[0], gi, gt
+    return loss[0], g[0], g[1]
 
 
 def solution(mesh):

time: 73.4 us -> 72.2 us (0.984)
  the two profiles are of different devices: /device:TPU:8 before, /device:TPU:64 now
where the time goes in v5:
time: 72.2 us; the launch traced here: 72 us
  Pallas kernels  66.8 us (93%)
  between operations  3.62 us (5%)
  local copies, waits for them, and re-layouts  1.63 us (2%)
    pallas_call x1, Pallas kernels, local(): pl.pallas_call(kernel, out_shape=(jax.ShapeDtypeStruct((1,), F32), jax.Sh...  66.8 us
    squeeze x1, local copies, waits for them, and re-layouts, local(): return (loss[0], g[0], g[1])  1.63 us

profile of v5, /device:TPU:64, one launch (start us, length us, event | category | flops | bytes accessed | tf_op | source)
XLA Modules:
  0.0 72.0 jit_solution(13191772582669443181)
XLA Ops:
  1.9 66.8 %shard_map.67 = (f32[1]{0:T(128)}, f32[2,28,768]{2,1,0:T(8,128)}) custom-call(f32[224,768]{1,0:T(8,128)} %img_hbm.1, f32[224,768]{1,0:T(8,128)} %txt_hbm.1, f32[1]{0:T(128)S(6)} %copy.8.lt_ref, f32[1]{0:T(128)S(6)} %copy.9.bias_ref), custom_call_target="tpu_custom_call" | custom-call | tf_op jit(solution)/shard_map/pallas_call | solution.py:454
  68.7 1.6 %slice_bitcast_fusion = (f32[28,768]{1,0:T(8,128)}, f32[28,768]{1,0:T(8,128)}) fusion(f32[2,28,768]{2,1,0:T(8,128)} %get-tuple-element.6), kind=kLoop, calls=%fused_computation | loop fusion | bytes 344064 | tf_op jit(solution)/shard_map/squeeze | solution.py:467

commit v6 on v5

--- a/solution.py
+++ b/solution.py
@@ -189,8 +189,8 @@
     offset = bias_ref[0]
     lacc[...] = jnp.zeros_like(lacc)
 
-    def pairs(t, half):
-        rows = slice(t * TT, (t + 1) * TT)
+    def pairs(start, n, half):
+        rows = slice(start, start + n)
         at = slice(half * S // 2, (half + 1) * S // 2)
         prod = dot3(yb_hi[rows, :], yb_lo[rows, :], xb_hi[at, :], xb_lo[at, :], 1, 1)
         logits = scale * prod + offset
@@ -199,7 +199,7 @@
         r = 1.0 / w
         sp = jnp.maximum(logits, 0.0) + (jnp.log(w) + (u - (w - 1.0)) * r)
         sig = jnp.where(logits >= 0.0, r, u * r)
-        lacc[...] += jnp.sum(sp.reshape(TT // 8, 8, S // 2), axis=0)
+        lacc[...] += jnp.sum(sp.reshape(n // 8, 8, S // 2), axis=0)
         hi, lo = split_bf16(sig)
         d_hi[rows, at] = hi
         d_lo[rows, at] = lo
@@ -233,18 +233,20 @@
     put_image(3, xs[2], 0)
     from_core(1)
     put_image(1, xc[1], 1)
-    pairs(0, 0)
+    pairs(0, TT, 0)
     from_x(2)
     from_core(3)
     put_image(3, xc[3], 1)
     put_image(2, xs[1], 0)
     from_core(2)
     put_image(2, xc[2], 1)
-    pairs(0, 1)
+    pairs(0, TT, 1)
+    for b in range(2):
+        pairs(TT, TT // 2, b)
     ag_take(4)
     put_text(3)
-    pairs(1, 0)
-    pairs(1, 1)
+    for b in range(2):
+        pairs(TT + TT // 2, TT // 2, b)
 
     sent = pl.ds(0, (NY - 1) * TEXT)
     rcopy(ys.at[sent, :], ys.at[sent, :], ag_ss, ag_rs.at[0], other).wait_send()

time: 72.2 us -> 72.9 us (level)
  no operation moved by 1% of the time
where the time goes in v6:
time: 72.9 us; the launch traced here: 72.7 us
  Pallas kernels  67.5 us (93%)
  between operations  3.62 us (5%)
  local copies, waits for them, and re-layouts  1.63 us (2%)
    pallas_call x1, Pallas kernels, local(): pl.pallas_call(kernel, out_shape=(jax.ShapeDtypeStruct((1,), F32), jax.Sh...  67.5 us
    squeeze x1, local copies, waits for them, and re-layouts, local(): return (loss[0], g[0], g[1])  1.63 us

profile of v6, /device:TPU:64, one launch (start us, length us, event | category | flops | bytes accessed | tf_op | source)
XLA Modules:
  0.0 72.7 jit_solution(3663032341737146008)
XLA Ops:
  1.9 67.5 %shard_map.67 = (f32[1]{0:T(128)}, f32[2,28,768]{2,1,0:T(8,128)}) custom-call(f32[224,768]{1,0:T(8,128)} %img_hbm.1, f32[224,768]{1,0:T(8,128)} %txt_hbm.1, f32[1]{0:T(128)S(6)} %copy.8.lt_ref, f32[1]{0:T(128)S(6)} %copy.9.bias_ref), custom_call_target="tpu_custom_call" | custom-call | tf_op jit(solution)/shard_map/pallas_call | solution.py:456
  69.4 1.6 %slice_bitcast_fusion = (f32[28,768]{1,0:T(8,128)}, f32[28,768]{1,0:T(8,128)}) fusion(f32[2,28,768]{2,1,0:T(8,128)} %get-tuple-element.6), kind=kLoop, calls=%fused_computation | loop fusion | bytes 344064 | tf_op jit(solution)/shard_map/squeeze | solution.py:469
